TPU v7x, 512 devices: a whole 4x8x8 slice. The times are simulated.
512 devices in a mesh: dp: 32 (over x, y), bucket: 16 (over z, core).
Axes of the slice: x: 4, y: 8, z: 8, core: 2. Of those that a mesh axis runs over, the one named last changes fastest.
Arguments:
- embeddings: float32 [65536, 256], P('dp'), may hold values from -40 to 40, as said below
- prototypes: float32 [16384, 256], P('bucket'), may hold values from -6 to 6, as said below
Outputs:
- new_protos: float32 [16384, 256], P('bucket')
- col_pot: float32 [16384], P('bucket')
Inputs may be any that keep to these rules, and one draw needn't show every extreme that they name: Real-valued embeddings. Real-valued prototypes.
All inputs are finite; a program needn't handle non-finite values.
Results may differ from a plain program's by a relative error of at most 0.0003.
Values sent between devices are 32-bit elements; how exact they have to be, the bound alone decides.
A program may use at most 64 MiB of HBM per device.

v0:
```python
import math

import jax
import jax.numpy as jnp
from jax import lax
from jax.sharding import PartitionSpec as P

ITERS = 3


def row_lse(shifted):
    peak = lax.pmax(jnp.max(shifted, axis=1), "bucket")
    mass = lax.psum(jnp.sum(jnp.exp(shifted - peak[:, None]), axis=1), "bucket")
    return peak + jnp.log(mass)


def col_lse(shifted):
    peak = lax.pmax(jnp.max(shifted, axis=0), "dp")
    mass = lax.psum(jnp.sum(jnp.exp(shifted - peak[None, :]), axis=0), "dp")
    return peak + jnp.log(mass)


def weighted_sum(weights, embeddings):
    return lax.dot_general(
        weights,
        embeddings,
        (((0,), (0,)), ((), ())),
        precision=lax.Precision.HIGHEST,
        preferred_element_type=jnp.float32,
    )


def normalize(centers):
    return centers * lax.rsqrt(jnp.mean(centers * centers, axis=1, keepdims=True) + 1e-06)


def body(embeddings, prototypes):
    width = embeddings.shape[1]
    local_protos = prototypes.shape[0]
    total_rows = embeddings.shape[0] * lax.axis_size("dp")
    total_protos = local_protos * lax.axis_size("bucket")
    logits = jnp.dot(
        embeddings,
        prototypes.T,
        precision=lax.Precision.HIGHEST,
        preferred_element_type=jnp.float32,
    ) * (2.0 / math.sqrt(width))
    col_pot = jnp.zeros((local_protos,), jnp.float32)
    row_pot = jnp.zeros((embeddings.shape[0],), jnp.float32)
    for step in range(ITERS):
        row_pot = -math.log(total_rows) - row_lse(logits + col_pot[None, :])
        col_pot = -math.log(total_protos) - col_lse(logits + row_pot[:, None])
    weights = jnp.exp(logits + row_pot[:, None] + col_pot[None, :])
    centers = lax.psum(weighted_sum(weights, embeddings), "dp") * float(total_protos)
    new_protos = normalize(centers)
    return (new_protos, col_pot)


def solution(mesh):
    in_specs = (P("dp", None), P("bucket", None))
    out_specs = (P("bucket", None), P("bucket"))
    return jax.shard_map(body, mesh=mesh, in_specs=in_specs, out_specs=out_specs, check_vma=False)
```

profile of v0, /device:TPU:1, one launch (start us, length us, event | category | flops | bytes accessed | tf_op | source)
XLA Modules:
  0.0 820.3 jit_solution(11348465038253309339)
XLA Ops:
  7.2 0.0 copy-start
  7.2 0.0 all-reduce.2.cloned.1.call-start
  7.2 1.5 copy-done
  8.8 10.4 %fusion.6 = (f32[2048]{0:T(1024)S(1)}, f32[2048,1024]{1,0:T(8,128)}) fusion(f32[2048,256]{1,0:T(8,128)S(1)} %copy-done, f32[1024,256]{1,0:T(8,128)} %param.3), kind=kOutput, calls=%fused_computation.27 | convolution fusion | flops 6446643200 | bytes 11542528 | tf_op jit(solution)/shard_map/dot_general | solution.py:42
  19.1 31.1 %pmax.42 = f32[2048]{0:T(1024)S(1)} all-reduce(f32[2048]{0:T(1024)S(1)} %get-tuple-element.2), channel_id=1, replica_groups=mesh['dp'=32,'bucket'=16] {'bucket'}, use_global_device_ids=true, to_apply=%region_1.0 | all-reduce | flops 2048 | bytes 16384 | tf_op jit(solution)/shard_map/pmax | solution.py:12
  50.2 4.4 exponential_reduce_fusion.5
  54.6 26.3 %psum.49 = f32[2048]{0:T(1024)S(1)} all-reduce(f32[2048]{0:T(1024)S(1)} %exponential_reduce_fusion.5), channel_id=1, replica_groups=mesh['dp'=32,'bucket'=16] {'bucket'}, use_global_device_ids=true, to_apply=%region_3.0 | all-reduce | flops 2048 | bytes 16384 | tf_op jit(solution)/shard_map/psum | solution.py:13
  81.0 4.0 add_reduce_fusion.3
  85.0 61.5 %pmax.43 = f32[1024]{0:T(1024)S(1)} all-reduce(f32[1024]{0:T(1024)S(1)} %add_reduce_fusion.3), channel_id=1, replica_groups=mesh['dp'=32,'bucket'=16] {'dp'}, use_global_device_ids=true, to_apply=%region_5.0 | all-reduce | flops 1024 | bytes 8192 | tf_op jit(solution)/shard_map/pmax | solution.py:18
  146.4 4.2 exponential_reduce_fusion.4
  150.7 55.7 %psum.50 = f32[1024]{0:T(1024)S(1)} all-reduce(f32[1024]{0:T(1024)S(1)} %exponential_reduce_fusion.4), channel_id=1, replica_groups=mesh['dp'=32,'bucket'=16] {'dp'}, use_global_device_ids=true, to_apply=%region_7.0 | all-reduce | flops 1024 | bytes 8192 | tf_op jit(solution)/shard_map/psum | solution.py:19
  206.4 4.0 add_reduce_fusion.2
  210.4 51.8 %pmax.44 = f32[2048]{0:T(1024)S(1)} all-reduce(f32[2048]{0:T(1024)S(1)} %add_reduce_fusion.2), channel_id=1, replica_groups=mesh['dp'=32,'bucket'=16] {'bucket'}, use_global_device_ids=true, to_apply=%region_9.0 | all-reduce | flops 2048 | bytes 16384 | tf_op jit(solution)/shard_map/pmax | solution.py:12
  262.2 4.3 exponential_reduce_fusion.3
  266.5 24.1 %psum.51 = f32[2048]{0:T(1024)S(1)} all-reduce(f32[2048]{0:T(1024)S(1)} %exponential_reduce_fusion.3), channel_id=1, replica_groups=mesh['dp'=32,'bucket'=16] {'bucket'}, use_global_device_ids=true, to_apply=%region_11.0 | all-reduce | flops 2048 | bytes 16384 | tf_op jit(solution)/shard_map/psum | solution.py:13
  290.6 4.0 add_reduce_fusion.1
  294.6 57.4 %pmax.45 = f32[1024]{0:T(1024)S(1)} all-reduce(f32[1024]{0:T(1024)S(1)} %add_reduce_fusion.1), channel_id=1, replica_groups=mesh['dp'=32,'bucket'=16] {'dp'}, use_global_device_ids=true, to_apply=%region_13.0 | all-reduce | flops 1024 | bytes 8192 | tf_op jit(solution)/shard_map/pmax | solution.py:18
  352.1 4.2 exponential_reduce_fusion.2
  356.3 56.1 %psum.52 = f32[1024]{0:T(1024)S(1)} all-reduce(f32[1024]{0:T(1024)S(1)} %exponential_reduce_fusion.2), channel_id=1, replica_groups=mesh['dp'=32,'bucket'=16] {'dp'}, use_global_device_ids=true, to_apply=%region_15.0 | all-reduce | flops 1024 | bytes 8192 | tf_op jit(solution)/shard_map/psum | solution.py:19
  412.4 4.0 add_reduce_fusion
  416.5 51.8 %pmax.46 = f32[2048]{0:T(1024)S(1)} all-reduce(f32[2048]{0:T(1024)S(1)} %add_reduce_fusion), channel_id=1, replica_groups=mesh['dp'=32,'bucket'=16] {'bucket'}, use_global_device_ids=true, to_apply=%region_17.0 | all-reduce | flops 2048 | bytes 16384 | tf_op jit(solution)/shard_map/pmax | solution.py:12
  468.2 4.3 exponential_reduce_fusion.1
  472.6 24.2 %psum.53 = f32[2048]{0:T(1024)S(1)} all-reduce(f32[2048]{0:T(1024)S(1)} %exponential_reduce_fusion.1), channel_id=1, replica_groups=mesh['dp'=32,'bucket'=16] {'bucket'}, use_global_device_ids=true, to_apply=%region_19.0 | all-reduce | flops 2048 | bytes 16384 | tf_op jit(solution)/shard_map/psum | solution.py:13
  496.8 4.0 add_reduce_fusion.4
  500.8 57.4 %pmax.47 = f32[1024]{0:T(1024)S(1)} all-reduce(f32[1024]{0:T(1024)S(1)} %add_reduce_fusion.4), channel_id=1, replica_groups=mesh['dp'=32,'bucket'=16] {'dp'}, use_global_device_ids=true, to_apply=%region_21.0 | all-reduce | flops 1024 | bytes 8192 | tf_op jit(solution)/shard_map/pmax | solution.py:18
  558.3 4.2 exponential_reduce_fusion
  562.5 56.1 %psum.54 = f32[1024]{0:T(1024)S(1)} all-reduce(f32[1024]{0:T(1024)S(1)} %exponential_reduce_fusion), channel_id=1, replica_groups=mesh['dp'=32,'bucket'=16] {'dp'}, use_global_device_ids=true, to_apply=%region_23.0 | all-reduce | flops 1024 | bytes 8192 | tf_op jit(solution)/shard_map/psum | solution.py:19
  618.7 0.0 copy-start.1
  618.7 17.2 %fusion = f32[1024,256]{1,0:T(8,128)} fusion(f32[2048,256]{1,0:T(8,128)S(1)} %copy-done, f32[2048,1024]{1,0:T(8,128)} %get-tuple-element.3, f32[1024]{0:T(1024)S(1)} %add_subtract_fusion.3, f32[2048]{0:T(1024)S(1)} %add_subtract_fusion), kind=kOutput, calls=%fused_computation | convolution fusion | flops 6446645248 | bytes 11546624 | tf_op jit(solution)/shard_map/dot_general | solution.py:24
  635.9 0.0 copy-done.1
  635.9 0.0 all-reduce.2.cloned.1.call-update
  635.9 173.7 %all-reduce.2.cloned.1.call-done = f32[1024,256]{1,0:T(8,128)} async-done(((f32[1024,256]{1,0:T(8,128)}), f32[1024,256]{1,0:T(8,128)}) %all-reduce.2.cloned.1.call-update) | async-done | bytes 1048592 | tf_op jit(solution)/shard_map/psum | solution.py:54
  809.6 1.4 multiply_reduce_fusion
  811.1 2.4 broadcast_multiply_fusion
  (7 shorter events, 0.1 us)
Async XLA Ops:
  7.2 1.6 copy-start
  7.2 802.4 %all-reduce.2.cloned.1.call-start = ((), (), s32[]{:S(2)}) async-start(), calls=%async_computation | async-start | bytes 2097152 | tf_op jit(solution)/shard_map/psum | solution.py:54
  618.7 17.2 %copy-start.1 = (f32[1024]{0:T(1024)}, f32[1024]{0:T(1024)S(1)}, u32[]{:S(2)}) copy-start(f32[1024]{0:T(1024)S(1)} %add_subtract_fusion.3) | copy-start | bytes 12292
Sparse Core Ops, SparseCore 0:
  636.0 173.5 all-reduce.1
where the time goes:
time: 824 us; the launch traced here: 820 us
  blocking collectives  554 us (67%)
  waiting for transfers between devices  174 us (21%)
  other arithmetic  49.7 us (6%)
  matrix products  27.6 us (3%)
  between operations  14.2 us (2%)
    pmax x3, blocking collectives, col_lse(): peak = lax.pmax(jnp.max(shifted, axis=0), 'dp')  176 us
    psum x1, waiting for transfers between devices, body(): lax.psum(weighted_sum(weights, embeddings), 'dp') * float(total_protos)  174 us
    psum x3, blocking collectives, col_lse(): mass = lax.psum(jnp.sum(jnp.exp(shifted - peak[None, :]), axis=0), 'dp')  168 us
    pmax x3, blocking collectives, row_lse(): peak = lax.pmax(jnp.max(shifted, axis=1), 'bucket')  135 us
    psum x3, blocking collectives, row_lse(): mass = lax.psum(jnp.sum(jnp.exp(shifted - peak[:, None]), axis=1), 'bucket')  74.6 us
    dot_general x1, matrix products, weighted_sum(): lax.dot_general(weights, embeddings, (((0,), (0,)), ((), ())), precision=...  17.2 us
  transfers between devices with their start and end apart: 1, of which 1 were waited for; matrix products, arithmetic and copies ran while one was open for 0% of the time, Pallas kernels for 0%

commit v1 on v0

v1 whole, which is shorter than its diff:
```python
import functools
import math

import jax
import jax.numpy as jnp
from jax import lax
from jax.experimental import pallas as pl
from jax.experimental.pallas import tpu as pltpu
from jax.sharding import PartitionSpec as P

NX, NY, NZ, NC = 4, 8, 8, 2
NDP = NX * NY
MESH = pl.DeviceIdType.MESH
F32 = jnp.float32
BF16 = jnp.bfloat16
LN2 = math.log(2.0)

ROWS = 2048
PROT = 1024
DW = 256
TOTAL_ROWS = ROWS * NDP
TOTAL_PROT = PROT * NZ * NC

XROWS = 768
XC1, XC2 = XROWS // NX, XROWS // NDP
YROWS = PROT - XROWS
YC1, YC2 = YROWS // NY, YROWS // NDP


def split(x):
    hi = x.astype(BF16)
    return hi, (x - hi.astype(F32)).astype(BF16)


def nt(a, b):
    return lax.dot_general(a, b, (((1,), (1,)), ((), ())), preferred_element_type=F32)


def nn(a, b):
    return lax.dot_general(a, b, (((1,), (0,)), ((), ())), preferred_element_type=F32)


def lanes(x, reduce):
    parts = [x[:, 128 * t : 128 * (t + 1)] for t in range(x.shape[1] // 128)]
    while len(parts) > 1:
        parts = [reduce(a, b) for a, b in zip(parts[::2], parts[1::2])]
    return parts[0]


def log_sum(terms):
    peak = functools.reduce(jnp.maximum, terms)
    mass = functools.reduce(jnp.add, [jnp.exp2(t - peak) for t in terms])
    return peak + jnp.log2(mass)


def total(terms):
    return functools.reduce(jnp.add, terms)


def kernel(
    e_hbm, p_hbm, cent_hbm, pot_ref,
    e_ref, p_ref, p3_ref, mat, hi_ref, lo_ref, sc_ref, part, wide, peaks, ewide, eh2, el2, lam,
    pair_buf, z_buf, xy_buf, vec_row, vec_col, sums, xb1, xb2, yb1, yb2, out,
    load_sem, ps, pr, zs, zr, cs, cr, fs, fr,
):
    dp, bk = lax.axis_index("dp"), lax.axis_index("bucket")
    x, y = dp // NY, dp % NY
    z, c = bk // NC, bk % NC

    load_p = pltpu.make_async_copy(p_hbm, p_ref, load_sem.at[0])
    load_e = pltpu.make_async_copy(e_hbm, e_ref, load_sem.at[1])
    load_p.start()
    load_e.start()

    pair_dev = (dp, z * NC + (1 - c))

    def z_dev(d):
        return (dp, ((z + d) % NZ) * NC + c)

    def xy_dev(dx, dy):
        return (((x + dx) % NX) * NY + (y + dy) % NY, bk)

    xy_peers = sorted(
        [(dx, dy) for dx in range(NX) for dy in range(NY) if dx or dy],
        key=lambda p: -(min(p[0], NX - p[0]) + min(p[1], NY - p[1])),
    )
    z_peers = sorted(range(1, NZ), key=lambda d: -min(d, NZ - d))
    x_peers, y_peers = [2, 1, 3], [4, 3, 5, 2, 6, 1, 7]

    barrier = pltpu.get_barrier_semaphore()
    everyone = [pair_dev] + [z_dev(d) for d in z_peers] + [xy_dev(*p) for p in xy_peers]
    for d in everyone:
        pl.semaphore_signal(barrier, 1, device_id=d, device_id_type=MESH)

    load_p.wait()
    ph, plo = split(p_ref[...] * F32(2.0 / math.sqrt(DW) / LN2))
    p3_ref[:, 0:DW] = ph
    p3_ref[:, DW : 2 * DW] = ph
    p3_ref[:, 2 * DW :] = plo
    load_e.wait()

    CH = 256

    def logits_chunk(j, _):
        r0 = pl.multiple_of(j * CH, CH)
        eh, el = split(e_ref[pl.ds(r0, CH), :])
        e3 = jnp.concatenate([eh, el, eh], axis=1)
        mat[:, pl.ds(r0, CH)] = nt(p3_ref[...], e3)

        def peak_step(g, m):
            return jnp.maximum(m, mat[pl.ds(pl.multiple_of(g * 8, 8), 8), pl.ds(r0, CH)])

        m = lax.fori_loop(0, PROT // 8, peak_step, jnp.full((8, CH), -jnp.inf, F32), unroll=16)
        m = jnp.max(m, axis=0, keepdims=True)

        def mass_step(g, s):
            return s + jnp.exp2(mat[pl.ds(pl.multiple_of(g * 8, 8), 8), pl.ds(r0, CH)] - m)

        s = lax.fori_loop(0, PROT // 8, mass_step, jnp.zeros((8, CH), F32), unroll=16)
        lam[:, pl.ds(r0, CH)] = m + jnp.log2(jnp.sum(s, axis=0, keepdims=True))
        return 0

    lax.fori_loop(0, ROWS // CH, logits_chunk, 0)

    pl.semaphore_wait(barrier, len(everyone))

    def row_exchange(n, vec, combine):
        vec_row[n] = vec
        cp = pltpu.make_async_remote_copy(
            vec_row.at[n], pair_buf.at[n], ps.at[n], pr.at[n], device_id=pair_dev, device_id_type=MESH)
        cp.start()
        cp.wait()
        mine = combine([vec, pair_buf[n]])
        z_buf[n, z] = mine
        for d in z_peers:
            pltpu.make_async_remote_copy(
                z_buf.at[n, z], z_buf.at[n, z], zs.at[n], zr.at[n], device_id=z_dev(d), device_id_type=MESH).start()
        seven = z_buf.at[n, pl.ds(0, NZ - 1)]
        pltpu.make_async_copy(seven, seven, zr.at[n]).wait()
        pltpu.make_async_copy(seven, seven, zs.at[n]).wait()
        return combine([z_buf[n, d] for d in range(NZ)])

    def col_send(n, vec):
        xy_buf[n, dp] = vec
        for p in xy_peers:
            pltpu.make_async_remote_copy(
                xy_buf.at[n, dp], xy_buf.at[n, dp], cs.at[n], cr.at[n], device_id=xy_dev(*p), device_id_type=MESH).start()

    def col_wait(n, combine):
        rest = xy_buf.at[n, pl.ds(0, NDP - 1)]
        pltpu.make_async_copy(rest, rest, cr.at[n]).wait()
        pltpu.make_async_copy(rest, rest, cs.at[n]).wait()
        return combine([xy_buf[n, d] for d in range(NDP)])

    def to_lanes(src, reduce):
        return jnp.concatenate(
            [reduce(src[128 * a : 128 * (a + 1), :].T, axis=0, keepdims=True) for a in range(PROT // 128)], axis=0)

    def to_wide(dst, vec, n):
        for a in range(n):
            dst[128 * a : 128 * (a + 1), :] = jnp.broadcast_to(vec[a : a + 1, :], (128, 128)).T

    def group(g):
        return pl.ds(pl.multiple_of(g * 8, 8), 8)

    def row_sums():
        def step(g, acc):
            v = wide[group(g), :]
            return acc + mat[group(g), :] * jnp.concatenate([v] * (ROWS // 128), axis=1)

        acc = lax.fori_loop(0, PROT // 8, step, jnp.zeros((8, ROWS), F32), unroll=4)
        return jnp.sum(acc, axis=0, keepdims=True)

    def col_sums(u):
        ub = jnp.broadcast_to(u, (8, ROWS))

        def step(g, _):
            part[group(g), :] = lanes(mat[group(g), :] * ub, jnp.add)
            return 0

        lax.fori_loop(0, PROT // 8, step, 0, unroll=4)
        return to_lanes(part, jnp.sum)

    r_log = row_exchange(0, lam[...], log_sum)

    rb = jnp.broadcast_to(r_log, (8, ROWS))

    def peak_group(g, _):
        part[group(g), :] = lanes(mat[group(g), :] - rb, jnp.maximum)
        return 0

    lax.fori_loop(0, PROT // 8, peak_group, 0, unroll=4)
    peak = to_lanes(part, jnp.max)
    to_wide(peaks, peak, PROT // 128)

    def exp_group(g, _):
        m = peaks[group(g), :]
        b = jnp.exp2(mat[group(g), :] - rb - jnp.concatenate([m] * (ROWS // 128), axis=1))
        mat[group(g), :] = b
        part[group(g), :] = lanes(b, jnp.add)
        return 0

    lax.fori_loop(0, PROT // 8, exp_group, 0, unroll=2)
    col_send(0, peak + jnp.log2(to_lanes(part, jnp.sum)))

    def halves(g, _):
        rows = pl.ds(pl.multiple_of(g * 16, 16), 16)
        h, l = split(mat[rows, :])
        hi_ref[rows, :] = h
        lo_ref[rows, :] = l
        return 0

    lax.fori_loop(0, PROT // 16, halves, 0, unroll=2)

    g_log = col_wait(0, log_sum)
    w = jnp.exp2(peak - g_log)
    ratio = TOTAL_ROWS / TOTAL_PROT
    to_wide(wide, w * ratio, PROT // 128)
    u = 1.0 / row_exchange(1, row_sums(), total)
    col_send(1, w * col_sums(u))
    mass = col_wait(1, total)
    to_wide(wide, w * ratio / mass, PROT // 128)
    u = 1.0 / row_exchange(2, row_sums(), total)

    vec_row[3] = u
    for a in range(ROWS // 128):
        ewide[128 * a : 128 * (a + 1), :] = jnp.broadcast_to(u[:, 128 * a : 128 * (a + 1)], (128, 128)).T
    to_wide(wide, w, PROT // 128)

    def scale_rows(g, _):
        rows = pl.ds(pl.multiple_of(g * 16, 16), 16)
        uw = ewide[rows, :]
        h, l = split(e_ref[rows, :] * jnp.concatenate([uw, uw], axis=1))
        eh2[rows, :] = h
        el2[rows, :] = l
        return 0

    lax.fori_loop(0, ROWS // 16, scale_rows, 0, unroll=4)

    def product(j, _):
        rows = pl.ds(pl.multiple_of(j * 256, 256), 256)
        h = hi_ref[rows, :]
        acc = nn(h, eh2[...]) + nn(h, el2[...]) + nn(lo_ref[rows, :], eh2[...])
        ww = wide[rows, :]
        sums[rows, :] = acc * jnp.concatenate([ww, ww], axis=1)
        return 0

    lax.fori_loop(0, PROT // 256, product, 0)

    def rows_of(base, unit, index):
        return pl.ds(pl.multiple_of(base + unit * index, 8), unit)

    def send(src, dst, n, device):
        pltpu.make_async_remote_copy(src, dst, fs.at[n], fr.at[n], device_id=device, device_id_type=MESH).start()

    def await_bytes(ref, sem):
        pltpu.make_async_copy(ref, ref, sem).wait()

    for d in x_peers:
        send(sums.at[rows_of(0, XC1, (x + d) % NX)], xb1.at[x], 0, xy_dev(d, 0))
    for d in y_peers:
        send(sums.at[rows_of(XROWS, YC1, (y + d) % NY)], yb1.at[y], 1, xy_dev(0, d))

    col_send(2, w * col_sums(u))

    xb1[x] = sums[rows_of(0, XC1, x), :]
    yb1[y] = sums[rows_of(XROWS, YC1, y), :]
    await_bytes(xb1.at[pl.ds(0, NX - 1)], fr.at[0])
    sc_ref[0:XC1, :] = total([xb1[d] for d in range(NX)])
    for d in y_peers:
        send(sc_ref.at[rows_of(0, XC2, (y + d) % NY)], xb2.at[y], 2, xy_dev(0, d))
    await_bytes(yb1.at[pl.ds(0, NY - 1)], fr.at[1])
    sc_ref[XC1 : XC1 + YC1, :] = total([yb1[d] for d in range(NY)])
    for d in x_peers:
        send(sc_ref.at[rows_of(XC1, YC2, (x + d) % NX)], yb2.at[x], 3, xy_dev(d, 0))

    mass = col_wait(2, total)
    pot_ref[...] = (math.log(TOTAL_ROWS / TOTAL_PROT) - LN2 * g_log) - jnp.log(mass)
    to_wide(part, 1.0 / mass, PROT // 128)

    def finish(terms, rows):
        s = part[rows, :]
        v = total(terms) * jnp.concatenate([s, s], axis=1)
        return v * lax.rsqrt(jnp.mean(v * v, axis=1, keepdims=True) + 1e-06)

    xb2[y] = sc_ref[rows_of(0, XC2, y), :]
    yb2[x] = sc_ref[rows_of(XC1, YC2, x), :]
    await_bytes(xb2.at[pl.ds(0, NY - 1)], fr.at[2])
    x_own = rows_of(0, XC2, x * NY + y)
    out[x_own, :] = finish([xb2[d] for d in range(NY)], x_own)
    for d in y_peers:
        send(out.at[x_own], out.at[x_own], 4, xy_dev(0, d))
    await_bytes(yb2.at[pl.ds(0, NX - 1)], fr.at[3])
    y_own = rows_of(XROWS, YC2, y * NX + x)
    out[y_own, :] = finish([yb2[d] for d in range(NX)], y_own)
    for d in x_peers:
        send(out.at[y_own], out.at[y_own], 5, xy_dev(d, 0))

    await_bytes(out.at[pl.ds(0, XC1 - XC2)], fr.at[4])
    x_mid = rows_of(0, XC1, x)
    for d in x_peers:
        send(out.at[x_mid], out.at[x_mid], 6, xy_dev(d, 0))
    await_bytes(out.at[pl.ds(0, YC1 - YC2)], fr.at[5])
    y_mid = rows_of(XROWS, YC1, y)
    for d in y_peers:
        send(out.at[y_mid], out.at[y_mid], 7, xy_dev(0, d))
    await_bytes(out.at[pl.ds(0, XROWS - XC1)], fr.at[6])
    await_bytes(out.at[pl.ds(0, YROWS - YC1)], fr.at[7])
    store = pltpu.make_async_copy(out, cent_hbm, load_sem.at[0])
    store.start()
    for n, size in enumerate((XROWS - XC1, YROWS - YC1, XC1 - XC2, YC1 - YC2, XC1 - XC2, YC1 - YC2, XROWS - XC1, YROWS - YC1)):
        await_bytes(out.at[pl.ds(0, size)], fs.at[n])
    store.wait()


def body(embeddings, prototypes):
    vm = pltpu.VMEM
    dma = pltpu.SemaphoreType.DMA
    new_protos, pot = pl.pallas_call(
        kernel,
        out_shape=(
            jax.ShapeDtypeStruct((PROT, DW), F32),
            jax.ShapeDtypeStruct((8, 128), F32),
        ),
        in_specs=[pl.BlockSpec(memory_space=pl.ANY)] * 2,
        out_specs=(pl.BlockSpec(memory_space=pl.ANY), pl.BlockSpec(memory_space=vm)),
        scratch_shapes=[
            vm((ROWS, DW), F32),
            vm((PROT, DW), F32),
            vm((PROT, 3 * DW), BF16),
            vm((PROT, ROWS), F32),
            vm((PROT, ROWS), BF16),
            vm((PROT, ROWS), BF16),
            vm((XC1 + YC1, DW), F32),
            vm((PROT, 128), F32),
            vm((PROT, 128), F32),
            vm((PROT, 128), F32),
            vm((ROWS, 128), F32),
            vm((ROWS, DW), BF16),
            vm((ROWS, DW), BF16),
            vm((1, ROWS), F32),
            vm((3, 1, ROWS), F32),
            vm((3, NZ, 1, ROWS), F32),
            vm((3, NDP, 8, 128), F32),
            vm((4, 1, ROWS), F32),
            vm((3, 8, 128), F32),
            vm((PROT, DW), F32),
            vm((NX, XC1, DW), F32),
            vm((NY, XC2, DW), F32),
            vm((NY, YC1, DW), F32),
            vm((NX, YC2, DW), F32),
            vm((PROT, DW), F32),
            dma((2,)),
            dma((3,)), dma((3,)),
            dma((3,)), dma((3,)),
            dma((3,)), dma((3,)),
            dma((8,)), dma((8,)),
        ],
        compiler_params=pltpu.CompilerParams(
            collective_id=0, has_side_effects=True, vmem_limit_bytes=56 * 1024 * 1024),
        name="sinkhorn",
    )(embeddings, prototypes)
    return new_protos, pot.reshape(PROT)


def solution(mesh):
    in_specs = (P("dp", None), P("bucket", None))
    out_specs = (P("bucket", None), P("bucket"))
    return jax.shard_map(body, mesh=mesh, in_specs=in_specs, out_specs=out_specs, check_vma=False)
```

time: 824 us -> 103 us (0.12)
  blocking collectives: 554 us -> 0 us
  waiting for transfers between devices: 174 us -> 0 us
  Pallas kernels: 0 us -> 97.7 us
  other arithmetic: 49.7 us -> 0 us
  matrix products: 27.6 us -> 0 us
  between operations: 14.2 us -> 0.65 us
    pmax x6 -> x0, blocking collectives: 311 us -> none  [the longest x3 176 us: col_lse(): peak = lax.pmax(jnp.max(shifted, axis=0), 'dp')]
    psum x6 -> x0, blocking collectives: 243 us -> none  [the longest x3 168 us: col_lse(): mass = lax.psum(jnp.sum(jnp.exp(shifted - peak[None, :]), axis=0), 'dp')]
    psum x1 -> x0, waiting for transfers between devices: 174 us -> none  [body(): lax.psum(weighted_sum(weights, embeddings), 'dp') * float(total_protos)]
    pallas_call x0 -> x1, Pallas kernels: none -> 97.7 us  [body(): pl.pallas_call(kernel, out_shape=(jax.ShapeDtypeStruct((PROT, DW), F32),...]
    dot_general x2 -> x0, matrix products: 27.6 us -> none  [the longest x1 17.2 us: weighted_sum(): lax.dot_general(weights, embeddings, (((0,), (0,)), ((), ())), precision=...]
    reduce_sum x7 -> x0, other arithmetic: 27.2 us -> none  [the longest x3 13.1 us: row_lse(): mass = lax.psum(jnp.sum(jnp.exp(shifted - peak[:, None]), axis=1), 'bucket')]
    reduce_max x5 -> x0, other arithmetic: 20 us -> none  [the longest x3 12 us: col_lse(): peak = lax.pmax(jnp.max(shifted, axis=0), 'dp')]
  transfers between devices with their start and end apart: 1 -> 0, of which waited for: 1 -> 0; matrix products, arithmetic and copies ran while one was open for 0% -> 0% of each run, Pallas kernels for 0% -> 0%
where the time goes in v1:
time: 103 us; the launch traced here: 101 us
  Pallas kernels  97.7 us (95%)
  local copies, waits for them, and re-layouts  2.86 us (3%)
    pallas_call x1, Pallas kernels, body(): pl.pallas_call(kernel, out_shape=(jax.ShapeDtypeStruct((PROT, DW), F32),...  97.7 us
    unnamed x4, local copies, waits for them, and re-layouts  2.86 us

profile of v1, /device:TPU:1, one launch (start us, length us, event | category | flops | bytes accessed | tf_op | source)
XLA Modules:
  0.0 101.2 jit_solution(9227014794265155206)
XLA Ops:
  0.6 97.7 %sinkhorn.1 = (f32[1024,256]{1,0:T(8,128)}, f32[8,128]{1,0:T(8,128)}) custom-call(f32[2048,256]{1,0:T(8,128)} %e_hbm.1, f32[1024,256]{1,0:T(8,128)} %p_hbm.1), custom_call_target="tpu_custom_call" | custom-call | tf_op jit(solution)/shard_map/sinkhorn/pallas_call | solution.py:319
  98.3 0.0 copy-start
  98.3 2.3 %copy.6 = f32[1024,256]{1,0:T(8,128)} copy(f32[1024,256]{1,0:T(8,128)} %get-tuple-element.8) | data formatting | bytes 2097152
  100.6 0.0 copy-done
  100.6 0.6 copy.7
Async XLA Ops:
  98.3 2.3 %copy-start = (f32[8,128]{1,0:T(8,128)S(1)}, f32[8,128]{1,0:T(8,128)}, u32[]{:S(2)}) copy-start(f32[8,128]{1,0:T(8,128)} %get-tuple-element.5) | copy-start | bytes 12292

commit v2 on v0

v2 whole, which is shorter than its diff:
```python
import functools
import math

import jax
import jax.numpy as jnp
from jax import lax
from jax.experimental import pallas as pl
from jax.experimental.pallas import tpu as pltpu
from jax.sharding import PartitionSpec as P

NX, NY, NZ, NC = 4, 8, 8, 2
NDP = NX * NY
MESH = pl.DeviceIdType.MESH
F32 = jnp.float32
BF16 = jnp.bfloat16
LN2 = math.log(2.0)

ROWS = 2048
PROT = 1024
DW = 256
TOTAL_ROWS = ROWS * NDP
TOTAL_PROT = PROT * NZ * NC

CH = 256
NCH = ROWS // CH
BLK = 64
PARTS = ((0, 256, "y"), (256, 256, "x"), (512, 256, "x"), (768, 256, "x"))


def split(x):
    hi = x.astype(BF16)
    return hi, (x - hi.astype(F32)).astype(BF16)


def nt(a, b):
    return lax.dot_general(a, b, (((1,), (1,)), ((), ())), preferred_element_type=F32)


def nn(a, b):
    return lax.dot_general(a, b, (((1,), (0,)), ((), ())), preferred_element_type=F32)


def tree(parts, op):
    while len(parts) > 1:
        parts = [op(a, b) for a, b in zip(parts[::2], parts[1::2])]
    return parts[0]


def twice(v):
    return jnp.concatenate([v, v], axis=1)


def fold(v, op):
    return op(v[:, :128], v[:, 128:])


def log_sum(terms):
    peak = functools.reduce(jnp.maximum, terms)
    mass = functools.reduce(jnp.add, [jnp.exp2(t - peak) for t in terms])
    return peak + jnp.log2(mass)


def total(terms):
    return functools.reduce(jnp.add, terms)


def kernel(*refs):
    (e_hbm, p_hbm, out, pot_ref, e_ref, p_ref, p3_ref), refs = refs[:7], refs[7:]
    mats, refs = refs[:NCH], refs[NCH:]
    b1s, refs = refs[: len(PARTS)], refs[len(PARTS) :]
    mids, refs = refs[: len(PARTS)], refs[len(PARTS) :]
    b2s, refs = refs[: len(PARTS)], refs[len(PARTS) :]
    (hi_ref, lo_ref, part, wide, peaks, ewide, eh2, el2, lam, rb_ref, pair_buf, z_buf, xy_buf, vec_row, sums,
     load_sem, ps, pr, zs, zr, cs, cr, fs, fr) = refs
    dp, bk = lax.axis_index("dp"), lax.axis_index("bucket")
    x, y = dp // NY, dp % NY
    z, c = bk // NC, bk % NC

    load_p = pltpu.make_async_copy(p_hbm, p_ref, load_sem.at[NCH])
    load_p.start()
    loads = []
    for j in range(NCH):
        rows = pl.ds(CH * j, CH)
        loads.append(pltpu.make_async_copy(e_hbm.at[rows], e_ref.at[rows], load_sem.at[j]))
        loads[-1].start()

    pair_dev = (dp, z * NC + (1 - c))

    def z_dev(d):
        return (dp, ((z + d) % NZ) * NC + c)

    def xy_dev(dx, dy):
        return (((x + dx) % NX) * NY + (y + dy) % NY, bk)

    xy_peers = sorted(
        [(dx, dy) for dx in range(NX) for dy in range(NY) if dx or dy],
        key=lambda p: -(min(p[0], NX - p[0]) + min(p[1], NY - p[1])),
    )
    z_peers = sorted(range(1, NZ), key=lambda d: -min(d, NZ - d))
    x_peers, y_peers = [2, 1, 3], [4, 3, 5, 2, 6, 1, 7]

    barrier = pltpu.get_barrier_semaphore()
    everyone = [pair_dev] + [z_dev(d) for d in z_peers] + [xy_dev(*p) for p in xy_peers]
    for d in everyone:
        pl.semaphore_signal(barrier, 1, device_id=d, device_id_type=MESH)

    load_p.wait()
    ph, plo = split(p_ref[...] * F32(2.0 / math.sqrt(DW) / LN2))
    p3_ref[:, 0:DW] = ph
    p3_ref[:, DW : 2 * DW] = ph
    p3_ref[:, 2 * DW :] = plo

    def deep(v, op):
        v = op(op(v.reshape(PROT // 32, 4, 8, CH), axis=0), axis=0)
        return op(v, axis=0, keepdims=True)

    for j in range(NCH + 1):
        if j < NCH:
            loads[j].wait()
            eh, el = split(e_ref[CH * j : CH * (j + 1), :])
            e3 = jnp.concatenate([eh, el, eh], axis=1)
            for q in range(0, PROT, 256):
                mats[j][q : q + 256, :] = nt(p3_ref[q : q + 256, :], e3)
        if j >= 1:
            v = mats[j - 1][...]
            m = deep(v, jnp.max)
            lam[:, CH * (j - 1) : CH * j] = m + jnp.log2(deep(jnp.exp2(v - m), jnp.sum))

    pl.semaphore_wait(barrier, len(everyone))

    def await_bytes(ref, sem):
        pltpu.make_async_copy(ref, ref, sem).wait()

    def send(src, dst, ssem, rsem, device):
        pltpu.make_async_remote_copy(src, dst, ssem, rsem, device_id=device, device_id_type=MESH).start()

    def row_exchange(n, vec, combine):
        vec_row[n] = vec
        send(vec_row.at[n], pair_buf.at[n], ps.at[n], pr.at[n], pair_dev)
        await_bytes(pair_buf.at[n], pr.at[n])
        z_buf[n, z] = combine([vec, pair_buf[n]])
        for d in z_peers:
            send(z_buf.at[n, z], z_buf.at[n, z], zs.at[n], zr.at[n], z_dev(d))
        await_bytes(vec_row.at[n], ps.at[n])
        seven = z_buf.at[n, pl.ds(0, NZ - 1)]
        await_bytes(seven, zr.at[n])
        await_bytes(seven, zs.at[n])
        return combine([z_buf[n, d] for d in range(NZ)])

    def col_send(n, vec):
        xy_buf[n, dp] = vec
        for p in xy_peers:
            send(xy_buf.at[n, dp], xy_buf.at[n, dp], cs.at[n], cr.at[n], xy_dev(*p))

    def col_wait(n, combine):
        rest = xy_buf.at[n, pl.ds(0, NDP - 1)]
        await_bytes(rest, cr.at[n])
        await_bytes(rest, cs.at[n])
        return combine([xy_buf[n, d] for d in range(NDP)])

    def to_lanes(src, reduce):
        return jnp.concatenate(
            [reduce(src[128 * a : 128 * (a + 1), :].T, axis=0, keepdims=True) for a in range(PROT // 128)], axis=0)

    def to_wide(dst, vec):
        for a in range(PROT // 128):
            dst[128 * a : 128 * (a + 1), :] = jnp.broadcast_to(vec[a : a + 1, :], (128, 128)).T

    def cut(j):
        return slice(CH * j, CH * (j + 1))

    def blocks(step, carry=0):
        return lax.fori_loop(
            0, PROT // BLK, lambda g, a: step(pl.ds(pl.multiple_of(g * BLK, BLK), BLK), a), carry)

    def row_sums():
        def step(r, acc):
            v = twice(wide[r, :])
            return tuple(a + jnp.sum((m[r, :] * v).reshape(BLK // 8, 8, CH), axis=0) for a, m in zip(acc, mats))

        acc = blocks(step, tuple(jnp.zeros((8, CH), F32) for _ in mats))
        return jnp.sum(jnp.concatenate(acc, axis=1), axis=0, keepdims=True)

    def col_sums(u):
        rb_ref[...] = u

        def step(r, a):
            part[r, :] = tree([fold(m[r, :] * rb_ref[:, cut(j)], jnp.add) for j, m in enumerate(mats)], jnp.add)
            return a

        blocks(step)
        return to_lanes(part, jnp.sum)

    rb_ref[...] = row_exchange(0, lam[...], log_sum)

    def peak_step(r, a):
        part[r, :] = tree([fold(m[r, :] - rb_ref[:, cut(j)], jnp.maximum) for j, m in enumerate(mats)], jnp.maximum)
        return a

    blocks(peak_step)
    peak = to_lanes(part, jnp.max)
    to_wide(peaks, peak)

    def exp_step(r, a):
        pk = twice(peaks[r, :])
        s = []
        for j, m in enumerate(mats):
            b = jnp.exp2(m[r, :] - rb_ref[:, cut(j)] - pk)
            m[r, :] = b
            s.append(fold(b, jnp.add))
        part[r, :] = tree(s, jnp.add)
        return a

    blocks(exp_step)
    col_send(0, peak + jnp.log2(to_lanes(part, jnp.sum)))

    def halves(r, a):
        for j, m in enumerate(mats):
            h, l = split(m[r, :])
            hi_ref[r, cut(j)] = h
            lo_ref[r, cut(j)] = l
        return a

    blocks(halves)

    g_log = col_wait(0, log_sum)
    w = jnp.exp2(peak - g_log)
    ratio = TOTAL_ROWS / TOTAL_PROT
    to_wide(wide, w * ratio)
    u = 1.0 / row_exchange(1, row_sums(), total)
    col_send(1, w * col_sums(u))
    mass = col_wait(1, total)
    to_wide(wide, w * ratio / mass)
    u = 1.0 / row_exchange(2, row_sums(), total)

    for a in range(ROWS // 128):
        ewide[128 * a : 128 * (a + 1), :] = jnp.broadcast_to(u[:, 128 * a : 128 * (a + 1)], (128, 128)).T
    to_wide(wide, w)

    def scale_rows(g, a):
        rows = pl.ds(pl.multiple_of(g * 128, 128), 128)
        h, l = split(e_ref[rows, :] * twice(ewide[rows, :]))
        eh2[rows, :] = h
        el2[rows, :] = l
        return a

    lax.fori_loop(0, ROWS // 128, scale_rows, 0)

    def rows_of(base, unit, index):
        return pl.ds(pl.multiple_of(base + unit * index, 8), unit)

    n_x, n_y = (NX, x, x_peers, lambda d: xy_dev(d, 0)), (NY, y, y_peers, lambda d: xy_dev(0, d))

    def plan(p):
        base, size, first = PARTS[p]
        one, two = (n_x, n_y) if first == "x" else (n_y, n_x)
        return base, size, one, two, size // one[0], size // NDP

    def scatter_one(p):
        base, size, (n, me, peers, dev), _, c1, _ = plan(p)
        for d in peers:
            send(sums.at[rows_of(base, c1, (me + d) % n)], b1s[p].at[me], fs.at[4 * p], fr.at[4 * p], dev(d))
        b1s[p][me] = sums[rows_of(base, c1, me), :]

    def scatter_two(p):
        _, size, (n1, _, _, _), (n, me, peers, dev), c1, c2 = plan(p)
        await_bytes(b1s[p].at[pl.ds(0, n1 - 1)], fr.at[4 * p])
        mids[p][...] = total([b1s[p][d] for d in range(n1)])
        for d in peers:
            send(mids[p].at[rows_of(0, c2, (me + d) % n)], b2s[p].at[me], fs.at[4 * p + 1], fr.at[4 * p + 1], dev(d))
        b2s[p][me] = mids[p][rows_of(0, c2, me), :]

    def gather_one(p):
        base, size, (_, me1, _, _), (n, me, peers, dev), c1, c2 = plan(p)
        await_bytes(b2s[p].at[pl.ds(0, n - 1)], fr.at[4 * p + 1])
        own = rows_of(base, c2, me1 * n + me)
        v = total([b2s[p][d] for d in range(n)]) * twice(part[own, :])
        out[own, :] = v * lax.rsqrt(jnp.mean(v * v, axis=1, keepdims=True) + 1e-06)
        for d in peers:
            send(out.at[own], out.at[own], fs.at[4 * p + 2], fr.at[4 * p + 2], dev(d))

    def gather_two(p):
        base, size, (_, me, peers, dev), _, c1, c2 = plan(p)
        await_bytes(out.at[pl.ds(0, c1 - c2)], fr.at[4 * p + 2])
        mid = rows_of(base, c1, me)
        for d in peers:
            send(out.at[mid], out.at[mid], fs.at[4 * p + 3], fr.at[4 * p + 3], dev(d))

    for p, (base, size, _) in enumerate(PARTS):
        rows = pl.ds(base, size)
        h = hi_ref[rows, :]
        acc = nn(h, eh2[...]) + nn(h, el2[...]) + nn(lo_ref[rows, :], eh2[...])
        sums[rows, :] = acc * twice(wide[rows, :])
        scatter_one(p)
        if p == 1:
            col_send(2, w * col_sums(u))

    scatter_two(1)
    scatter_two(2)
    scatter_two(0)
    scatter_two(3)
    mass = col_wait(2, total)
    pot_ref[...] = ((math.log(TOTAL_ROWS / TOTAL_PROT) - LN2 * g_log) - jnp.log(mass)).reshape(pot_ref.shape)
    to_wide(part, 1.0 / mass)
    for p in (1, 0, 2, 3):
        gather_one(p)
    for p in (0, 1, 2, 3):
        gather_two(p)
    for p in (0, 1, 2, 3):
        _, size, _, _, c1, c2 = plan(p)
        await_bytes(out.at[pl.ds(0, size - c1)], fr.at[4 * p + 3])
        for n, sent in enumerate((size - c1, c1 - c2, c1 - c2, size - c1)):
            await_bytes(sums.at[pl.ds(0, sent)], fs.at[4 * p + n])


def body(embeddings, prototypes):
    vm = pltpu.VMEM
    dma = pltpu.SemaphoreType.DMA
    counts = [(NX, NY) if first == "x" else (NY, NX) for _, _, first in PARTS]
    sizes = [size for _, size, _ in PARTS]
    new_protos, pot = pl.pallas_call(
        kernel,
        out_shape=(pltpu.VMEM((PROT, DW), F32), pltpu.VMEM((PROT,), F32)),
        in_specs=[pl.BlockSpec(memory_space=pl.ANY)] * 2,
        out_specs=(pl.BlockSpec(memory_space=vm), pl.BlockSpec(memory_space=vm)),
        scratch_shapes=[
            vm((ROWS, DW), F32),
            vm((PROT, DW), F32),
            vm((PROT, 3 * DW), BF16),
            *[vm((PROT, CH), F32) for _ in range(NCH)],
            *[vm((a, s // a, DW), F32) for (a, _), s in zip(counts, sizes)],
            *[vm((s // a, DW), F32) for (a, _), s in zip(counts, sizes)],
            *[vm((b, s // NDP, DW), F32) for (_, b), s in zip(counts, sizes)],
            vm((PROT, ROWS), BF16),
            vm((PROT, ROWS), BF16),
            vm((PROT, 128), F32),
            vm((PROT, 128), F32),
            vm((PROT, 128), F32),
            vm((ROWS, 128), F32),
            vm((ROWS, DW), BF16),
            vm((ROWS, DW), BF16),
            vm((1, ROWS), F32),
            vm((1, ROWS), F32),
            vm((3, 1, ROWS), F32),
            vm((3, NZ, 1, ROWS), F32),
            vm((3, NDP, 8, 128), F32),
            vm((3, 1, ROWS), F32),
            vm((PROT, DW), F32),
            dma((NCH + 1,)),
            dma((3,)), dma((3,)),
            dma((3,)), dma((3,)),
            dma((3,)), dma((3,)),
            dma((4 * len(PARTS),)), dma((4 * len(PARTS),)),
        ],
        compiler_params=pltpu.CompilerParams(
            collective_id=0, has_side_effects=True, vmem_limit_bytes=56 * 1024 * 1024),
        name="sinkhorn",
    )(embeddings, prototypes)
    return new_protos, pot


def solution(mesh):
    in_specs = (P("dp", None), P("bucket", None))
    out_specs = (P("bucket", None), P("bucket"))
    return jax.shard_map(body, mesh=mesh, in_specs=in_specs, out_specs=out_specs, check_vma=False)
```

time: 824 us -> 86.7 us (0.11)
  blocking collectives: 554 us -> 0 us
  waiting for transfers between devices: 174 us -> 0 us
  Pallas kernels: 0 us -> 83.4 us
  other arithmetic: 49.7 us -> 0 us
  matrix products: 27.6 us -> 0 us
  between operations: 14.2 us -> 0.64 us
    pmax x6 -> x0, blocking collectives: 311 us -> none  [the longest x3 176 us: col_lse(): peak = lax.pmax(jnp.max(shifted, axis=0), 'dp')]
    psum x6 -> x0, blocking collectives: 243 us -> none  [the longest x3 168 us: col_lse(): mass = lax.psum(jnp.sum(jnp.exp(shifted - peak[None, :]), axis=0), 'dp')]
    psum x1 -> x0, waiting for transfers between devices: 174 us -> none  [body(): lax.psum(weighted_sum(weights, embeddings), 'dp') * float(total_protos)]
    pallas_call x0 -> x1, Pallas kernels: none -> 83.4 us  [body(): pl.pallas_call(kernel, out_shape=(pltpu.VMEM((PROT, DW), F32), pltpu.VMEM...]
    dot_general x2 -> x0, matrix products: 27.6 us -> none  [the longest x1 17.2 us: weighted_sum(): lax.dot_general(weights, embeddings, (((0,), (0,)), ((), ())), precision=...]
    reduce_sum x7 -> x0, other arithmetic: 27.2 us -> none  [the longest x3 13.1 us: row_lse(): mass = lax.psum(jnp.sum(jnp.exp(shifted - peak[:, None]), axis=1), 'bucket')]
    reduce_max x5 -> x0, other arithmetic: 20 us -> none  [the longest x3 12 us: col_lse(): peak = lax.pmax(jnp.max(shifted, axis=0), 'dp')]
  transfers between devices with their start and end apart: 1 -> 0, of which waited for: 1 -> 0; matrix products, arithmetic and copies ran while one was open for 0% -> 0% of each run, Pallas kernels for 0% -> 0%
where the time goes in v2:
time: 86.7 us; the launch traced here: 85.6 us
  Pallas kernels  83.4 us (96%)
  local copies, waits for them, and re-layouts  1.57 us (2%)
    pallas_call x1, Pallas kernels, body(): pl.pallas_call(kernel, out_shape=(pltpu.VMEM((PROT, DW), F32), pltpu.VMEM...  83.4 us

profile of v2, /device:TPU:1, one launch (start us, length us, event | category | flops | bytes accessed | tf_op | source)
XLA Modules:
  0.0 85.6 jit_solution(532810593203792099)
XLA Ops:
  0.6 83.4 %sinkhorn.1 = (f32[1024,256]{1,0:T(8,128)S(1)}, f32[1024]{0:T(1024)S(1)}) custom-call(f32[2048,256]{1,0:T(8,128)} %refs_0_.1, f32[1024,256]{1,0:T(8,128)} %refs_1_.1), custom_call_target="tpu_custom_call" | custom-call | tf_op jit(solution)/shard_map/sinkhorn/pallas_call | solution.py:321
  84.0 1.0 %copy.6 = f32[1024,256]{1,0:T(8,128)} copy(f32[1024,256]{1,0:T(8,128)S(1)} %get-tuple-element.2) | data formatting | bytes 2097152
  85.0 0.6 copy.7

commit v3 on v2

v3 whole, which is shorter than its diff:
```python
import functools
import math

import jax
import jax.numpy as jnp
from jax import lax
from jax.experimental import pallas as pl
from jax.experimental.pallas import tpu as pltpu
from jax.sharding import PartitionSpec as P

NX, NY, NZ, NC = 4, 8, 8, 2
NDP = NX * NY
MESH = pl.DeviceIdType.MESH
F32 = jnp.float32
BF16 = jnp.bfloat16
LN2 = math.log(2.0)

ROWS = 2048
PROT = 1024
DW = 256
TOTAL_ROWS = ROWS * NDP
TOTAL_PROT = PROT * NZ * NC

CH = 256
NCH = ROWS // CH
HALF = ROWS // 2
NB = NZ * NC
PARTS = ((0, 256, "y"), (256, 256, "x"), (512, 256, "x"), (768, 256, "x"))


def split(x):
    hi = x.astype(BF16)
    return hi, (x - hi.astype(F32)).astype(BF16)


def nt(a, b):
    return lax.dot_general(a, b, (((1,), (1,)), ((), ())), preferred_element_type=F32)


def nn(a, b):
    return lax.dot_general(a, b, (((1,), (0,)), ((), ())), preferred_element_type=F32)


def tree(parts, op):
    while len(parts) > 1:
        parts = [op(a, b) for a, b in zip(parts[::2], parts[1::2])]
    return parts[0]


def twice(v):
    return jnp.concatenate([v, v], axis=1)


def fold(v, op):
    return op(v[:, :128], v[:, 128:])


def log_sum(terms):
    peak = functools.reduce(jnp.maximum, terms)
    mass = functools.reduce(jnp.add, [jnp.exp2(t - peak) for t in terms])
    return peak + jnp.log2(mass)


def total(terms):
    return functools.reduce(jnp.add, terms)


def kernel(*refs):
    (e_hbm, p_hbm, out, pot_ref, e_ref, p_ref, p3_ref), refs = refs[:7], refs[7:]
    mats, refs = refs[:NCH], refs[NCH:]
    b1s, refs = refs[: len(PARTS)], refs[len(PARTS) :]
    mids, refs = refs[: len(PARTS)], refs[len(PARTS) :]
    b2s, refs = refs[: len(PARTS)], refs[len(PARTS) :]
    (hi_ref, lo_ref, part, wide, peaks, eh2, el2, lam, rb_ref, z_buf, xy_buf, c3x, c3y, sums,
     load_sem, zs, zr, cs, cr, fs, fr) = refs
    dp, bk = lax.axis_index("dp"), lax.axis_index("bucket")
    x, y = dp // NY, dp % NY
    z, c = bk // NC, bk % NC

    loads_e, loads_p = [], []
    for j in range(NCH):
        rows = pl.ds(CH * j, CH)
        loads_e.append(pltpu.make_async_copy(e_hbm.at[rows], e_ref.at[rows], load_sem.at[j]))
    for q in range(PROT // CH):
        rows = pl.ds(CH * q, CH)
        loads_p.append(pltpu.make_async_copy(p_hbm.at[rows], p_ref.at[rows], load_sem.at[NCH + q]))
    for copy in loads_e[:1] + loads_p + loads_e[1:]:
        copy.start()

    def bk_dev(d):
        return (dp, (bk + d) % NB)

    def xy_dev(dx, dy):
        return (((x + dx) % NX) * NY + (y + dy) % NY, bk)

    xy_peers = sorted(
        [(dx, dy) for dx in range(NX) for dy in range(NY) if dx or dy],
        key=lambda p: -(min(p[0], NX - p[0]) + min(p[1], NY - p[1])),
    )
    bk_peers = sorted(range(1, NB), key=lambda d: -min(d, NB - d))
    x_peers, y_peers = [2, 1, 3], [4, 3, 5, 2, 6, 1, 7]

    barrier = pltpu.get_barrier_semaphore()
    everyone = [bk_dev(d) for d in bk_peers] + [xy_dev(*p) for p in xy_peers]
    for d in everyone:
        pl.semaphore_signal(barrier, 1, device_id=d, device_id_type=MESH)

    def await_bytes(ref, sem):
        pltpu.make_async_copy(ref, ref, sem).wait()

    def send(src, dst, ssem, rsem, device):
        pltpu.make_async_remote_copy(src, dst, ssem, rsem, device_id=device, device_id_type=MESH).start()

    def row_send(n, h, vec):
        z_buf[n, h, bk] = vec
        for d in bk_peers:
            send(z_buf.at[n, h, bk], z_buf.at[n, h, bk], zs.at[2 * n + h], zr.at[2 * n + h], bk_dev(d))

    def row_wait(n, h, combine):
        rest = z_buf.at[n, h, pl.ds(0, NB - 1)]
        await_bytes(rest, zr.at[2 * n + h])
        await_bytes(rest, zs.at[2 * n + h])
        return combine([z_buf[n, h, d] for d in range(NB)])

    def deep(v, op):
        v = op(op(v.reshape(PROT // 32, 4, 8, CH), axis=0), axis=0)
        return op(v, axis=0, keepdims=True)

    for j in range(NCH + 1):
        if j < NCH:
            loads_e[j].wait()
            eh, el = split(e_ref[CH * j : CH * (j + 1), :])
            e3 = jnp.concatenate([eh, el, eh], axis=1)
            for q in range(PROT // CH):
                r = slice(CH * q, CH * (q + 1))
                if j == 0:
                    loads_p[q].wait()
                    ph, plo = split(p_ref[r, :] * F32(2.0 / math.sqrt(DW) / LN2))
                    p3_ref[r, 0:DW] = ph
                    p3_ref[r, DW : 2 * DW] = ph
                    p3_ref[r, 2 * DW :] = plo
                mats[j][r, :] = nt(p3_ref[r, :], e3)
        if j >= 1:
            v = mats[j - 1][...]
            m = deep(v, jnp.max)
            lam[:, CH * (j - 1) : CH * j] = m + jnp.log2(deep(jnp.exp2(v - m), jnp.sum))
        if j == NCH // 2:
            pl.semaphore_wait(barrier, len(everyone))
            row_send(0, 0, lam[:, :HALF])
    row_send(0, 1, lam[:, HALF:])

    def col_send(n, vec):
        xy_buf[n, dp] = vec
        for p in xy_peers:
            send(xy_buf.at[n, dp], xy_buf.at[n, dp], cs.at[n], cr.at[n], xy_dev(*p))

    def col_wait(n, combine):
        rest = xy_buf.at[n, pl.ds(0, NDP - 1)]
        await_bytes(rest, cr.at[n])
        await_bytes(rest, cs.at[n])
        return combine([xy_buf[n, d] for d in range(NDP)])

    def to_row(v, reduce):
        return reduce(v.T, axis=0, keepdims=True)

    def to_tile(row):
        return jnp.broadcast_to(row, (128, 128)).T

    def cut(j):
        return slice(CH * j, CH * (j + 1))

    blocks = [slice(128 * a, 128 * (a + 1)) for a in range(PROT // 128)]
    groups = (range(NCH // 2), range(NCH // 2, NCH))

    def half(h):
        return slice(HALF * h, HALF * (h + 1))

    def row_sums(h, vec=None):
        acc = [jnp.zeros((8, CH), F32) for _ in groups[h]]
        for a, r in enumerate(blocks):
            if vec is not None:
                wide[r, :] = to_tile(vec[a : a + 1, :])
            v = twice(wide[r, :])
            acc = [t + jnp.sum((mats[j][r, :] * v).reshape(16, 8, CH), axis=0) for t, j in zip(acc, groups[h])]
        return jnp.sum(jnp.concatenate(acc, axis=1), axis=0, keepdims=True)

    def row_step(n, vec):
        row_send(n, 0, row_sums(0, vec))
        row_send(n, 1, row_sums(1))

    def col_terms(r, js):
        return tree([fold(mats[j][r, :] * rb_ref[:, cut(j)], jnp.add) for j in js], jnp.add)

    def peak_terms(r, js):
        return tree([fold(mats[j][r, :] - rb_ref[:, cut(j)], jnp.maximum) for j in js], jnp.maximum)

    rb_ref[:, half(0)] = row_wait(0, 0, log_sum)
    for r in blocks:
        part[r, :] = peak_terms(r, groups[0])
    rb_ref[:, half(1)] = row_wait(0, 1, log_sum)
    rows_of_peaks = []
    for r in blocks:
        row = to_row(jnp.maximum(part[r, :], peak_terms(r, groups[1])), jnp.max)
        rows_of_peaks.append(row)
        peaks[r, :] = to_tile(row)
    peak = jnp.concatenate(rows_of_peaks, axis=0)

    masses = []
    for r in blocks:
        pk = twice(peaks[r, :])
        terms = []
        for j, m in enumerate(mats):
            b = jnp.exp2(m[r, :] - rb_ref[:, cut(j)] - pk)
            m[r, :] = b
            terms.append(fold(b, jnp.add))
        masses.append(to_row(tree(terms, jnp.add), jnp.sum))
    col_send(0, peak + jnp.log2(jnp.concatenate(masses, axis=0)))

    def halves(g, carry):
        r = pl.ds(pl.multiple_of(g * 64, 64), 64)
        for j, m in enumerate(mats):
            h, l = split(m[r, :])
            hi_ref[r, cut(j)] = h
            lo_ref[r, cut(j)] = l
        return carry

    lax.fori_loop(0, PROT // 64, halves, 0)

    g_log = col_wait(0, log_sum)
    w = jnp.exp2(peak - g_log)
    ratio = TOTAL_ROWS / TOTAL_PROT
    row_step(1, w * ratio)
    for a, r in enumerate(blocks):
        peaks[r, :] = to_tile(w[a : a + 1, :])
    rb_ref[:, half(0)] = 1.0 / row_wait(1, 0, total)
    for r in blocks:
        part[r, :] = col_terms(r, groups[0])
    rb_ref[:, half(1)] = 1.0 / row_wait(1, 1, total)
    col_send(1, w * jnp.concatenate([to_row(part[r, :] + col_terms(r, groups[1]), jnp.sum) for r in blocks], axis=0))
    row_step(2, w * ratio / col_wait(1, total))

    def scale_rows(h):
        for a in range(8 * h, 8 * h + 8):
            r = slice(128 * a, 128 * (a + 1))
            t, l = split(e_ref[r, :] * twice(to_tile(rb_ref[:, r])))
            eh2[r, :] = t
            el2[r, :] = l

    def product(r, k):
        h = hi_ref[r, k]
        return nn(h, eh2[k, :]) + nn(h, el2[k, :]) + nn(lo_ref[r, k], eh2[k, :])

    rb_ref[:, half(0)] = 1.0 / row_wait(2, 0, total)
    scale_rows(0)
    first = slice(PARTS[0][0], PARTS[0][0] + PARTS[0][1])
    sums[first, :] = product(first, half(0))
    rb_ref[:, half(1)] = 1.0 / row_wait(2, 1, total)
    scale_rows(1)

    def rows_of(base, unit, index):
        return pl.ds(pl.multiple_of(base + unit * index, 8), unit)

    n_x, n_y = (NX, x, x_peers, lambda d: xy_dev(d, 0)), (NY, y, y_peers, lambda d: xy_dev(0, d))

    def plan(p):
        base, size, first = PARTS[p]
        one, two = (n_x, n_y) if first == "x" else (n_y, n_x)
        return base, size, one, two, size // one[0], size // NDP

    def scatter_one(p):
        base, size, (n, me, peers, dev), _, c1, _ = plan(p)
        for d in peers:
            send(sums.at[rows_of(base, c1, (me + d) % n)], b1s[p].at[me], fs.at[4 * p], fr.at[4 * p], dev(d))
        b1s[p][me] = sums[rows_of(base, c1, me), :]

    def scatter_two(p):
        _, size, (n1, _, _, _), (n, me, peers, dev), c1, c2 = plan(p)
        await_bytes(b1s[p].at[pl.ds(0, n1 - 1)], fr.at[4 * p])
        mids[p][...] = total([b1s[p][d] for d in range(n1)])
        for d in peers:
            send(mids[p].at[rows_of(0, c2, (me + d) % n)], b2s[p].at[me], fs.at[4 * p + 1], fr.at[4 * p + 1], dev(d))
        b2s[p][me] = mids[p][rows_of(0, c2, me), :]

    def gather_one(p):
        base, size, (_, me1, _, _), (n, me, peers, dev), c1, c2 = plan(p)
        await_bytes(b2s[p].at[pl.ds(0, n - 1)], fr.at[4 * p + 1])
        own = rows_of(base, c2, me1 * n + me)
        v = total([b2s[p][d] for d in range(n)]) * twice(part[own, :])
        out[own, :] = v * lax.rsqrt(jnp.mean(v * v, axis=1, keepdims=True) + 1e-06)
        for d in peers:
            send(out.at[own], out.at[own], fs.at[4 * p + 2], fr.at[4 * p + 2], dev(d))

    def gather_two(p):
        base, size, (_, me, peers, dev), _, c1, c2 = plan(p)
        await_bytes(out.at[pl.ds(0, c1 - c2)], fr.at[4 * p + 2])
        mid = rows_of(base, c1, me)
        for d in peers:
            send(out.at[mid], out.at[mid], fs.at[4 * p + 3], fr.at[4 * p + 3], dev(d))

    for p, (base, size, _) in enumerate(PARTS):
        rows = slice(base, base + size)
        acc = sums[rows, :] + product(rows, half(1)) if p == 0 else product(rows, slice(0, ROWS))
        sums[rows, :] = acc * twice(peaks[rows, :])
        scatter_one(p)
        if p == 1:
            c3x[x] = w * jnp.concatenate([to_row(col_terms(r, range(NCH)), jnp.sum) for r in blocks], axis=0)
            for d in x_peers:
                send(c3x.at[x], c3x.at[x], cs.at[2], cr.at[2], xy_dev(d, 0))

    scatter_two(1)
    await_bytes(c3x.at[pl.ds(0, NX - 1)], cr.at[2])
    c3y[y] = total([c3x[d] for d in range(NX)])
    for d in y_peers:
        send(c3y.at[y], c3y.at[y], cs.at[3], cr.at[3], xy_dev(0, d))
    scatter_two(2)
    scatter_two(0)
    scatter_two(3)
    await_bytes(c3y.at[pl.ds(0, NY - 1)], cr.at[3])
    mass = total([c3y[d] for d in range(NY)])
    pot_ref[...] = ((math.log(TOTAL_ROWS / TOTAL_PROT) - LN2 * g_log) - jnp.log(mass)).reshape(pot_ref.shape)
    for a, r in enumerate(blocks):
        part[r, :] = to_tile(1.0 / mass[a : a + 1, :])
    await_bytes(c3x.at[pl.ds(0, NX - 1)], cs.at[2])
    await_bytes(c3y.at[pl.ds(0, NY - 1)], cs.at[3])
    for p in (1, 0, 2, 3):
        gather_one(p)
    for p in (0, 1, 2, 3):
        gather_two(p)
    for p in (0, 1, 2, 3):
        _, size, _, _, c1, c2 = plan(p)
        await_bytes(out.at[pl.ds(0, size - c1)], fr.at[4 * p + 3])
        for n, sent in enumerate((size - c1, c1 - c2, c1 - c2, size - c1)):
            await_bytes(sums.at[pl.ds(0, sent)], fs.at[4 * p + n])


def body(embeddings, prototypes):
    vm = pltpu.VMEM
    dma = pltpu.SemaphoreType.DMA
    counts = [(NX, NY) if first == "x" else (NY, NX) for _, _, first in PARTS]
    sizes = [size for _, size, _ in PARTS]
    new_protos, pot = pl.pallas_call(
        kernel,
        out_shape=(pltpu.VMEM((PROT, DW), F32), pltpu.VMEM((PROT,), F32)),
        in_specs=[pl.BlockSpec(memory_space=pl.ANY)] * 2,
        out_specs=(pl.BlockSpec(memory_space=vm), pl.BlockSpec(memory_space=vm)),
        scratch_shapes=[
            vm((ROWS, DW), F32),
            vm((PROT, DW), F32),
            vm((PROT, 3 * DW), BF16),
            *[vm((PROT, CH), F32) for _ in range(NCH)],
            *[vm((a, s // a, DW), F32) for (a, _), s in zip(counts, sizes)],
            *[vm((s // a, DW), F32) for (a, _), s in zip(counts, sizes)],
            *[vm((b, s // NDP, DW), F32) for (_, b), s in zip(counts, sizes)],
            vm((PROT, ROWS), BF16),
            vm((PROT, ROWS), BF16),
            vm((PROT, 128), F32),
            vm((PROT, 128), F32),
            vm((PROT, 128), F32),
            vm((ROWS, DW), BF16),
            vm((ROWS, DW), BF16),
            vm((1, ROWS), F32),
            vm((1, ROWS), F32),
            vm((3, 2, NB, 1, HALF), F32),
            vm((2, NDP, 8, 128), F32),
            vm((NX, 8, 128), F32),
            vm((NY, 8, 128), F32),
            vm((PROT, DW), F32),
            dma((NCH + PROT // CH,)),
            dma((6,)), dma((6,)),
            dma((4,)), dma((4,)),
            dma((4 * len(PARTS),)), dma((4 * len(PARTS),)),
        ],
        compiler_params=pltpu.CompilerParams(
            collective_id=0, has_side_effects=True, vmem_limit_bytes=56 * 1024 * 1024),
        name="sinkhorn",
    )(embeddings, prototypes)
    return new_protos, pot


def solution(mesh):
    in_specs = (P("dp", None), P("bucket", None))
    out_specs = (P("bucket", None), P("bucket"))
    return jax.shard_map(body, mesh=mesh, in_specs=in_specs, out_specs=out_specs, check_vma=False)
```

time: 86.7 us -> 81.9 us (0.945)
  Pallas kernels: 83.4 us -> 78.6 us
    pallas_call x1, Pallas kernels: 83.4 us -> 78.6 us  [body(): pl.pallas_call(kernel, out_shape=(pltpu.VMEM((PROT, DW), F32), pltpu.VMEM...]
where the time goes in v3:
time: 81.9 us; the launch traced here: 80.8 us
  Pallas kernels  78.6 us (96%)
  local copies, waits for them, and re-layouts  1.57 us (2%)
    pallas_call x1, Pallas kernels, body(): pl.pallas_call(kernel, out_shape=(pltpu.VMEM((PROT, DW), F32), pltpu.VMEM...  78.6 us

profile of v3, /device:TPU:1, one launch (start us, length us, event | category | flops | bytes accessed | tf_op | source)
XLA Modules:
  0.0 80.8 jit_solution(10306771289992942244)
XLA Ops:
  0.6 78.6 %sinkhorn.1 = (f32[1024,256]{1,0:T(8,128)S(1)}, f32[1024]{0:T(1024)S(1)}) custom-call(f32[2048,256]{1,0:T(8,128)} %refs_0_.1, f32[1024,256]{1,0:T(8,128)} %refs_1_.1), custom_call_target="tpu_custom_call" | custom-call | tf_op jit(solution)/shard_map/sinkhorn/pallas_call | solution.py:341
  79.2 1.0 %copy.6 = f32[1024,256]{1,0:T(8,128)} copy(f32[1024,256]{1,0:T(8,128)S(1)} %get-tuple-element.2) | data formatting | bytes 2097152
  80.2 0.6 copy.7

commit v4 on v3

--- a/solution.py
+++ b/solution.py
@@ -25,7 +25,7 @@
 NCH = ROWS // CH
 HALF = ROWS // 2
 NB = NZ * NC
-PARTS = ((0, 256, "y"), (256, 256, "x"), (512, 256, "x"), (768, 256, "x"))
+PARTS = ((0, 256, "y"), (256, 256, "x"), (512, 256, "x"), (768, 128, "x"), (896, 128, "x"))
 
 
 def split(x):
@@ -71,7 +71,7 @@
     b1s, refs = refs[: len(PARTS)], refs[len(PARTS) :]
     mids, refs = refs[: len(PARTS)], refs[len(PARTS) :]
     b2s, refs = refs[: len(PARTS)], refs[len(PARTS) :]
-    (hi_ref, lo_ref, part, wide, peaks, eh2, el2, lam, rb_ref, z_buf, xy_buf, c3x, c3y, sums,
+    (hi_ref, lo_ref, part, wide, peaks, eh2, el2, lam, rb_ref, z_buf, xy_buf, c3x, c3y, sums, raw,
      load_sem, zs, zr, cs, cr, fs, fr) = refs
     dp, bk = lax.axis_index("dp"), lax.axis_index("bucket")
     x, y = dp // NY, dp % NY
@@ -265,72 +265,92 @@
     def plan(p):
         base, size, first = PARTS[p]
         one, two = (n_x, n_y) if first == "x" else (n_y, n_x)
-        return base, size, one, two, size // one[0], size // NDP
+        return base, size, one, two, size // one[0]
+
+    def piece(base, c1, n, index):
+        if c1 == 8 * n:
+            return rows_of(base, 8, index), pl.ds(0, DW)
+        return rows_of(base, 8, index // 2), pl.ds(pl.multiple_of(128 * (index % 2), 128), 128)
 
     def scatter_one(p):
-        base, size, (n, me, peers, dev), _, c1, _ = plan(p)
+        base, size, (n, me, peers, dev), _, c1 = plan(p)
         for d in peers:
             send(sums.at[rows_of(base, c1, (me + d) % n)], b1s[p].at[me], fs.at[4 * p], fr.at[4 * p], dev(d))
         b1s[p][me] = sums[rows_of(base, c1, me), :]
 
     def scatter_two(p):
-        _, size, (n1, _, _, _), (n, me, peers, dev), c1, c2 = plan(p)
+        _, size, (n1, _, _, _), (n, me, peers, dev), c1 = plan(p)
         await_bytes(b1s[p].at[pl.ds(0, n1 - 1)], fr.at[4 * p])
         mids[p][...] = total([b1s[p][d] for d in range(n1)])
         for d in peers:
-            send(mids[p].at[rows_of(0, c2, (me + d) % n)], b2s[p].at[me], fs.at[4 * p + 1], fr.at[4 * p + 1], dev(d))
-        b2s[p][me] = mids[p][rows_of(0, c2, me), :]
+            send(mids[p].at[piece(0, c1, n, (me + d) % n)], b2s[p].at[me], fs.at[4 * p + 1], fr.at[4 * p + 1], dev(d))
+        b2s[p][me] = mids[p][piece(0, c1, n, me)]
 
     def gather_one(p):
-        base, size, (_, me1, _, _), (n, me, peers, dev), c1, c2 = plan(p)
+        base, size, (_, me1, _, _), (n, me, peers, dev), c1 = plan(p)
         await_bytes(b2s[p].at[pl.ds(0, n - 1)], fr.at[4 * p + 1])
-        own = rows_of(base, c2, me1 * n + me)
-        v = total([b2s[p][d] for d in range(n)]) * twice(part[own, :])
-        out[own, :] = v * lax.rsqrt(jnp.mean(v * v, axis=1, keepdims=True) + 1e-06)
+        own = piece(base + c1 * me1, c1, n, me)
+        raw[own] = total([b2s[p][d] for d in range(n)])
         for d in peers:
-            send(out.at[own], out.at[own], fs.at[4 * p + 2], fr.at[4 * p + 2], dev(d))
+            send(raw.at[own], raw.at[own], fs.at[4 * p + 2], fr.at[4 * p + 2], dev(d))
 
     def gather_two(p):
-        base, size, (_, me, peers, dev), _, c1, c2 = plan(p)
-        await_bytes(out.at[pl.ds(0, c1 - c2)], fr.at[4 * p + 2])
+        base, size, (_, me, peers, dev), (n, _, _, _), c1 = plan(p)
+        await_bytes(b2s[p].at[pl.ds(0, n - 1)], fr.at[4 * p + 2])
         mid = rows_of(base, c1, me)
         for d in peers:
-            send(out.at[mid], out.at[mid], fs.at[4 * p + 3], fr.at[4 * p + 3], dev(d))
+            send(raw.at[mid], raw.at[mid], fs.at[4 * p + 3], fr.at[4 * p + 3], dev(d))
+
+    def finish(p):
+        base, size, (n1, _, _, _), _, c1 = plan(p)
+        await_bytes(sums.at[pl.ds(0, size - c1)], fr.at[4 * p + 3])
+        rows = slice(base, base + size)
+        v = raw[rows, :] * twice(part[rows, :])
+        out[rows, :] = v * lax.rsqrt(jnp.mean(v * v, axis=1, keepdims=True) + 1e-06)
 
     for p, (base, size, _) in enumerate(PARTS):
         rows = slice(base, base + size)
         acc = sums[rows, :] + product(rows, half(1)) if p == 0 else product(rows, slice(0, ROWS))
         sums[rows, :] = acc * twice(peaks[rows, :])
         scatter_one(p)
-        if p == 1:
-            c3x[x] = w * jnp.concatenate([to_row(col_terms(r, range(NCH)), jnp.sum) for r in blocks], axis=0)
-            for d in x_peers:
-                send(c3x.at[x], c3x.at[x], cs.at[2], cr.at[2], xy_dev(d, 0))
+
+    c3x[x] = w * jnp.concatenate([to_row(col_terms(r, range(NCH)), jnp.sum) for r in blocks], axis=0)
+    for d in x_peers:
+        send(c3x.at[x], c3x.at[x], cs.at[2], cr.at[2], xy_dev(d, 0))
 
     scatter_two(1)
+    scatter_two(2)
+    scatter_two(0)
     await_bytes(c3x.at[pl.ds(0, NX - 1)], cr.at[2])
     c3y[y] = total([c3x[d] for d in range(NX)])
     for d in y_peers:
         send(c3y.at[y], c3y.at[y], cs.at[3], cr.at[3], xy_dev(0, d))
-    scatter_two(2)
-    scatter_two(0)
     scatter_two(3)
+    scatter_two(4)
+    gather_one(1)
+    gather_one(0)
+    gather_one(2)
+    gather_two(0)
+    gather_one(3)
+    gather_one(4)
+    gather_two(1)
     await_bytes(c3y.at[pl.ds(0, NY - 1)], cr.at[3])
     mass = total([c3y[d] for d in range(NY)])
     pot_ref[...] = ((math.log(TOTAL_ROWS / TOTAL_PROT) - LN2 * g_log) - jnp.log(mass)).reshape(pot_ref.shape)
     for a, r in enumerate(blocks):
         part[r, :] = to_tile(1.0 / mass[a : a + 1, :])
+    gather_two(2)
+    gather_two(3)
+    gather_two(4)
+    for p in range(len(PARTS)):
+        finish(p)
     await_bytes(c3x.at[pl.ds(0, NX - 1)], cs.at[2])
     await_bytes(c3y.at[pl.ds(0, NY - 1)], cs.at[3])
-    for p in (1, 0, 2, 3):
-        gather_one(p)
-    for p in (0, 1, 2, 3):
-        gather_two(p)
-    for p in (0, 1, 2, 3):
-        _, size, _, _, c1, c2 = plan(p)
-        await_bytes(out.at[pl.ds(0, size - c1)], fr.at[4 * p + 3])
-        for n, sent in enumerate((size - c1, c1 - c2, c1 - c2, size - c1)):
-            await_bytes(sums.at[pl.ds(0, sent)], fs.at[4 * p + n])
+    for p in range(len(PARTS)):
+        _, size, _, (n, _, _, _), c1 = plan(p)
+        for k in range(4):
+            sent = b2s[p].at[pl.ds(0, n - 1)] if k in (1, 2) else sums.at[pl.ds(0, size - c1)]
+            await_bytes(sent, fs.at[4 * p + k])
 
 
 def body(embeddings, prototypes):
@@ -350,7 +370,7 @@
             *[vm((PROT, CH), F32) for _ in range(NCH)],
             *[vm((a, s // a, DW), F32) for (a, _), s in zip(counts, sizes)],
             *[vm((s // a, DW), F32) for (a, _), s in zip(counts, sizes)],
-            *[vm((b, s // NDP, DW), F32) for (_, b), s in zip(counts, sizes)],
+            *[vm((b, 8, s // NDP * DW // 8), F32) for (_, b), s in zip(counts, sizes)],
             vm((PROT, ROWS), BF16),
             vm((PROT, ROWS), BF16),
             vm((PROT, 128), F32),
@@ -365,6 +385,7 @@
             vm((NX, 8, 128), F32),
             vm((NY, 8, 128), F32),
             vm((PROT, DW), F32),
+            vm((PROT, DW), F32),
             dma((NCH + PROT // CH,)),
             dma((6,)), dma((6,)),
             dma((4,)), dma((4,)),

time: 81.9 us -> 86.1 us (1.051)
  Pallas kernels: 78.6 us -> 83.3 us
    pallas_call x1, Pallas kernels: 78.6 us -> 83.3 us  [body(): pl.pallas_call(kernel, out_shape=(pltpu.VMEM((PROT, DW), F32), pltpu.VMEM...]
where the time goes in v4:
time: 86.1 us; the launch traced here: 85.5 us
  Pallas kernels  83.3 us (97%)
  local copies, waits for them, and re-layouts  1.57 us (2%)
    pallas_call x1, Pallas kernels, body(): pl.pallas_call(kernel, out_shape=(pltpu.VMEM((PROT, DW), F32), pltpu.VMEM...  83.3 us

profile of v4, /device:TPU:1, one launch (start us, length us, event | category | flops | bytes accessed | tf_op | source)
XLA Modules:
  0.0 85.5 jit_solution(13104478516487512819)
XLA Ops:
  0.6 83.3 %sinkhorn.1 = (f32[1024,256]{1,0:T(8,128)S(1)}, f32[1024]{0:T(1024)S(1)}) custom-call(f32[2048,256]{1,0:T(8,128)} %refs_0_.1, f32[1024,256]{1,0:T(8,128)} %refs_1_.1), custom_call_target="tpu_custom_call" | custom-call | tf_op jit(solution)/shard_map/sinkhorn/pallas_call | solution.py:361
  84.0 1.0 %copy.6 = f32[1024,256]{1,0:T(8,128)} copy(f32[1024,256]{1,0:T(8,128)S(1)} %get-tuple-element.2) | data formatting | bytes 2097152
  84.9 0.6 copy.7

commit v5 on v3

--- a/solution.py
+++ b/solution.py
@@ -1,4 +1,3 @@
-import functools
 import math
 
 import jax
@@ -56,13 +55,13 @@
 
 
 def log_sum(terms):
-    peak = functools.reduce(jnp.maximum, terms)
-    mass = functools.reduce(jnp.add, [jnp.exp2(t - peak) for t in terms])
+    peak = tree(terms, jnp.maximum)
+    mass = tree([jnp.exp2(t - peak) for t in terms], jnp.add)
     return peak + jnp.log2(mass)
 
 
 def total(terms):
-    return functools.reduce(jnp.add, terms)
+    return tree(terms, jnp.add)
 
 
 def kernel(*refs):
@@ -71,11 +70,10 @@
     b1s, refs = refs[: len(PARTS)], refs[len(PARTS) :]
     mids, refs = refs[: len(PARTS)], refs[len(PARTS) :]
     b2s, refs = refs[: len(PARTS)], refs[len(PARTS) :]
-    (hi_ref, lo_ref, part, wide, peaks, eh2, el2, lam, rb_ref, z_buf, xy_buf, c3x, c3y, sums,
-     load_sem, zs, zr, cs, cr, fs, fr) = refs
+    (hi_ref, lo_ref, part, wide, peaks, eh2, el2, rb_ref, z_buf, xy_buf, c3x, c3y, sums,
+     load_sem, zs, zr, cs, cr, fs, fr, gr) = refs
     dp, bk = lax.axis_index("dp"), lax.axis_index("bucket")
-    x, y = dp // NY, dp % NY
-    z, c = bk // NC, bk % NC
+    x, y = lax.div(dp, NY), lax.rem(dp, NY)
 
     loads_e, loads_p = [], []
     for j in range(NCH):
@@ -88,10 +86,10 @@
         copy.start()
 
     def bk_dev(d):
-        return (dp, (bk + d) % NB)
+        return (dp, lax.rem(bk + d, NB))
 
     def xy_dev(dx, dy):
-        return (((x + dx) % NX) * NY + (y + dy) % NY, bk)
+        return (lax.rem(x + dx, NX) * NY + lax.rem(y + dy, NY), bk)
 
     xy_peers = sorted(
         [(dx, dy) for dx in range(NX) for dy in range(NY) if dx or dy],
@@ -126,6 +124,7 @@
         v = op(op(v.reshape(PROT // 32, 4, 8, CH), axis=0), axis=0)
         return op(v, axis=0, keepdims=True)
 
+    lams = []
     for j in range(NCH + 1):
         if j < NCH:
             loads_e[j].wait()
@@ -143,11 +142,13 @@
         if j >= 1:
             v = mats[j - 1][...]
             m = deep(v, jnp.max)
-            lam[:, CH * (j - 1) : CH * j] = m + jnp.log2(deep(jnp.exp2(v - m), jnp.sum))
+            lam = m + jnp.log2(deep(jnp.exp2(v - m), jnp.sum))
+            lams += [lam[:, :128], lam[:, 128:]]
         if j == NCH // 2:
             pl.semaphore_wait(barrier, len(everyone))
-            row_send(0, 0, lam[:, :HALF])
-    row_send(0, 1, lam[:, HALF:])
+            row_send(0, 0, jnp.concatenate(lams, axis=0))
+            lams = []
+    row_send(0, 1, jnp.concatenate(lams, axis=0))
 
     def col_send(n, vec):
         xy_buf[n, dp] = vec
@@ -174,6 +175,10 @@
 
     def half(h):
         return slice(HALF * h, HALF * (h + 1))
+
+    def spread(h, vec):
+        for t in range(8):
+            rb_ref[:, HALF * h + 128 * t : HALF * h + 128 * (t + 1)] = vec[t : t + 1, :]
 
     def row_sums(h, vec=None):
         acc = [jnp.zeros((8, CH), F32) for _ in groups[h]]
@@ -182,7 +187,8 @@
                 wide[r, :] = to_tile(vec[a : a + 1, :])
             v = twice(wide[r, :])
             acc = [t + jnp.sum((mats[j][r, :] * v).reshape(16, 8, CH), axis=0) for t, j in zip(acc, groups[h])]
-        return jnp.sum(jnp.concatenate(acc, axis=1), axis=0, keepdims=True)
+        return jnp.concatenate(
+            [jnp.sum(t[:, k : k + 128], axis=0, keepdims=True) for t in acc for k in (0, 128)], axis=0)
 
     def row_step(n, vec):
         row_send(n, 0, row_sums(0, vec))
@@ -194,10 +200,10 @@
     def peak_terms(r, js):
         return tree([fold(mats[j][r, :] - rb_ref[:, cut(j)], jnp.maximum) for j in js], jnp.maximum)
 
-    rb_ref[:, half(0)] = row_wait(0, 0, log_sum)
+    spread(0, row_wait(0, 0, log_sum))
     for r in blocks:
         part[r, :] = peak_terms(r, groups[0])
-    rb_ref[:, half(1)] = row_wait(0, 1, log_sum)
+    spread(1, row_wait(0, 1, log_sum))
     rows_of_peaks = []
     for r in blocks:
         row = to_row(jnp.maximum(part[r, :], peak_terms(r, groups[1])), jnp.max)
@@ -232,10 +238,10 @@
     row_step(1, w * ratio)
     for a, r in enumerate(blocks):
         peaks[r, :] = to_tile(w[a : a + 1, :])
-    rb_ref[:, half(0)] = 1.0 / row_wait(1, 0, total)
+    spread(0, 1.0 / row_wait(1, 0, total))
     for r in blocks:
         part[r, :] = col_terms(r, groups[0])
-    rb_ref[:, half(1)] = 1.0 / row_wait(1, 1, total)
+    spread(1, 1.0 / row_wait(1, 1, total))
     col_send(1, w * jnp.concatenate([to_row(part[r, :] + col_terms(r, groups[1]), jnp.sum) for r in blocks], axis=0))
     row_step(2, w * ratio / col_wait(1, total))
 
@@ -250,11 +256,11 @@
         h = hi_ref[r, k]
         return nn(h, eh2[k, :]) + nn(h, el2[k, :]) + nn(lo_ref[r, k], eh2[k, :])
 
-    rb_ref[:, half(0)] = 1.0 / row_wait(2, 0, total)
+    spread(0, 1.0 / row_wait(2, 0, total))
     scale_rows(0)
     first = slice(PARTS[0][0], PARTS[0][0] + PARTS[0][1])
     sums[first, :] = product(first, half(0))
-    rb_ref[:, half(1)] = 1.0 / row_wait(2, 1, total)
+    spread(1, 1.0 / row_wait(2, 1, total))
     scale_rows(1)
 
     def rows_of(base, unit, index):
@@ -270,7 +276,7 @@
     def scatter_one(p):
         base, size, (n, me, peers, dev), _, c1, _ = plan(p)
         for d in peers:
-            send(sums.at[rows_of(base, c1, (me + d) % n)], b1s[p].at[me], fs.at[4 * p], fr.at[4 * p], dev(d))
+            send(sums.at[rows_of(base, c1, lax.rem(me + d, n))], b1s[p].at[me], fs.at[4 * p], fr.at[4 * p], dev(d))
         b1s[p][me] = sums[rows_of(base, c1, me), :]
 
     def scatter_two(p):
@@ -278,7 +284,7 @@
         await_bytes(b1s[p].at[pl.ds(0, n1 - 1)], fr.at[4 * p])
         mids[p][...] = total([b1s[p][d] for d in range(n1)])
         for d in peers:
-            send(mids[p].at[rows_of(0, c2, (me + d) % n)], b2s[p].at[me], fs.at[4 * p + 1], fr.at[4 * p + 1], dev(d))
+            send(mids[p].at[rows_of(0, c2, lax.rem(me + d, n))], b2s[p].at[me], fs.at[4 * p + 1], fr.at[4 * p + 1], dev(d))
         b2s[p][me] = mids[p][rows_of(0, c2, me), :]
 
     def gather_one(p):
@@ -288,14 +294,25 @@
         v = total([b2s[p][d] for d in range(n)]) * twice(part[own, :])
         out[own, :] = v * lax.rsqrt(jnp.mean(v * v, axis=1, keepdims=True) + 1e-06)
         for d in peers:
-            send(out.at[own], out.at[own], fs.at[4 * p + 2], fr.at[4 * p + 2], dev(d))
+            arrived = fr.at[4 * p + 2] if PARTS[p][2] == "y" else gr.at[NY * p + d]
+            send(out.at[own], out.at[own], fs.at[4 * p + 2], arrived, dev(d))
+        if PARTS[p][2] == "x":
+            for d in x_peers:
+                send(out.at[own], out.at[own], fs.at[4 * p + 3], fr.at[4 * p + 3], xy_dev(d, 0))
 
     def gather_two(p):
         base, size, (_, me, peers, dev), _, c1, c2 = plan(p)
-        await_bytes(out.at[pl.ds(0, c1 - c2)], fr.at[4 * p + 2])
-        mid = rows_of(base, c1, me)
-        for d in peers:
-            send(out.at[mid], out.at[mid], fs.at[4 * p + 3], fr.at[4 * p + 3], dev(d))
+        if PARTS[p][2] == "y":
+            await_bytes(out.at[pl.ds(0, c1 - c2)], fr.at[4 * p + 2])
+            mid = rows_of(base, c1, me)
+            for d in peers:
+                send(out.at[mid], out.at[mid], fs.at[4 * p + 3], fr.at[4 * p + 3], dev(d))
+            return
+        for e in (1, 7, 2, 6, 3, 5, 4):
+            got = rows_of(base + c1 * x, c2, lax.rem(y + NY - e, NY))
+            await_bytes(out.at[got], gr.at[NY * p + e])
+            for d in x_peers:
+                send(out.at[got], out.at[got], fs.at[4 * p + 3], fr.at[4 * p + 3], xy_dev(d, 0))
 
     for p, (base, size, _) in enumerate(PARTS):
         rows = slice(base, base + size)
@@ -359,8 +376,7 @@
             vm((ROWS, DW), BF16),
             vm((ROWS, DW), BF16),
             vm((1, ROWS), F32),
-            vm((1, ROWS), F32),
-            vm((3, 2, NB, 1, HALF), F32),
+            vm((3, 2, NB, 8, 128), F32),
             vm((2, NDP, 8, 128), F32),
             vm((NX, 8, 128), F32),
             vm((NY, 8, 128), F32),
@@ -368,7 +384,7 @@
             dma((NCH + PROT // CH,)),
             dma((6,)), dma((6,)),
             dma((4,)), dma((4,)),
-            dma((4 * len(PARTS),)), dma((4 * len(PARTS),)),
+            dma((4 * len(PARTS),)), dma((4 * len(PARTS),)), dma((NY * len(PARTS),)),
         ],
         compiler_params=pltpu.CompilerParams(
             collective_id=0, has_side_effects=True, vmem_limit_bytes=56 * 1024 * 1024),

time: 81.9 us -> 82 us (level); the launches traced: 80.8 us -> 81.9 us
  Pallas kernels: 78.6 us -> 79.7 us
    pallas_call x1, Pallas kernels: 78.6 us -> 79.7 us  [body(): pl.pallas_call(kernel, out_shape=(pltpu.VMEM((PROT, DW), F32), pltpu.VMEM...]
where the time goes in v5:
time: 82 us; the launch traced here: 81.9 us
  Pallas kernels  79.7 us (97%)
  local copies, waits for them, and re-layouts  1.57 us (2%)
    pallas_call x1, Pallas kernels, body(): pl.pallas_call(kernel, out_shape=(pltpu.VMEM((PROT, DW), F32), pltpu.VMEM...  79.7 us

profile of v5, /device:TPU:1, one launch (start us, length us, event | category | flops | bytes accessed | tf_op | source)
XLA Modules:
  0.0 81.9 jit_solution(16379098310487299329)
XLA Ops:
  0.6 79.7 %sinkhorn.1 = (f32[1024,256]{1,0:T(8,128)S(1)}, f32[1024]{0:T(1024)S(1)}) custom-call(f32[2048,256]{1,0:T(8,128)} %refs_0_.1, f32[1024,256]{1,0:T(8,128)} %refs_1_.1), custom_call_target="tpu_custom_call" | custom-call | tf_op jit(solution)/shard_map/sinkhorn/pallas_call | solution.py:358
  80.3 1.0 %copy.6 = f32[1024,256]{1,0:T(8,128)} copy(f32[1024,256]{1,0:T(8,128)S(1)} %get-tuple-element.2) | data formatting | bytes 2097152
  81.3 0.6 copy.7

commit v6 on v5

--- a/solution.py
+++ b/solution.py
@@ -117,7 +117,6 @@
     def row_wait(n, h, combine):
         rest = z_buf.at[n, h, pl.ds(0, NB - 1)]
         await_bytes(rest, zr.at[2 * n + h])
-        await_bytes(rest, zs.at[2 * n + h])
         return combine([z_buf[n, h, d] for d in range(NB)])
 
     def deep(v, op):
@@ -158,7 +157,6 @@
     def col_wait(n, combine):
         rest = xy_buf.at[n, pl.ds(0, NDP - 1)]
         await_bytes(rest, cr.at[n])
-        await_bytes(rest, cs.at[n])
         return combine([xy_buf[n, d] for d in range(NDP)])
 
     def to_row(v, reduce):
@@ -337,8 +335,6 @@
     pot_ref[...] = ((math.log(TOTAL_ROWS / TOTAL_PROT) - LN2 * g_log) - jnp.log(mass)).reshape(pot_ref.shape)
     for a, r in enumerate(blocks):
         part[r, :] = to_tile(1.0 / mass[a : a + 1, :])
-    await_bytes(c3x.at[pl.ds(0, NX - 1)], cs.at[2])
-    await_bytes(c3y.at[pl.ds(0, NY - 1)], cs.at[3])
     for p in (1, 0, 2, 3):
         gather_one(p)
     for p in (0, 1, 2, 3):
@@ -348,6 +344,21 @@
         await_bytes(out.at[pl.ds(0, size - c1)], fr.at[4 * p + 3])
         for n, sent in enumerate((size - c1, c1 - c2, c1 - c2, size - c1)):
             await_bytes(sums.at[pl.ds(0, sent)], fs.at[4 * p + n])
+
+    for n in range(2):
+        await_bytes(xy_buf.at[n, pl.ds(0, NDP - 1)], cs.at[n])
+    for n in range(6):
+        await_bytes(z_buf.at[n // 2, n % 2, pl.ds(0, NB - 1)], zs.at[n])
+    await_bytes(c3x.at[pl.ds(0, NX - 1)], cs.at[2])
+    await_bytes(c3y.at[pl.ds(0, NY - 1)], cs.at[3])
+
+
+def store(a, b, a_out, b_out, sems):
+    copies = [pltpu.make_async_copy(a, a_out, sems.at[0]), pltpu.make_async_copy(b, b_out, sems.at[1])]
+    for copy in copies:
+        copy.start()
+    for copy in copies:
+        copy.wait()
 
 
 def body(embeddings, prototypes):
@@ -390,7 +401,14 @@
             collective_id=0, has_side_effects=True, vmem_limit_bytes=56 * 1024 * 1024),
         name="sinkhorn",
     )(embeddings, prototypes)
-    return new_protos, pot
+    return pl.pallas_call(
+        store,
+        out_shape=(jax.ShapeDtypeStruct((PROT, DW), F32), jax.ShapeDtypeStruct((PROT,), F32)),
+        in_specs=[pl.BlockSpec(memory_space=pl.ANY)] * 2,
+        out_specs=(pl.BlockSpec(memory_space=pl.ANY), pl.BlockSpec(memory_space=pl.ANY)),
+        scratch_shapes=[dma((2,))],
+        name="store",
+    )(new_protos, pot)
 
 
 def solution(mesh):

time: 82 us -> 115 us (1.40)
  Pallas kernels: 79.7 us -> 113 us
    pallas_call x0 -> x1, Pallas kernels: none -> 33 us  [body(): pl.pallas_call(store, out_shape=(jax.ShapeDtypeStruct((PROT, DW), F32), j...]
where the time goes in v6:
time: 115 us
  Pallas kernels  113 us (98%)
  local copies, waits for them, and re-layouts  1.56 us (1%)
    pallas_call x1, Pallas kernels, body(): pl.pallas_call(kernel, out_shape=(pltpu.VMEM((PROT, DW), F32), pltpu.VMEM...  79.6 us
    pallas_call x1, Pallas kernels, body(): pl.pallas_call(store, out_shape=(jax.ShapeDtypeStruct((PROT, DW), F32), j...  33 us

profile of v6, /device:TPU:1, one launch (start us, length us, event | category | flops | bytes accessed | tf_op | source)
XLA Modules:
  0.0 115.0 jit_solution(14975637163118850375)
XLA Ops:
  0.6 79.6 %sinkhorn.1 = (f32[1024,256]{1,0:T(8,128)S(1)}, f32[1024]{0:T(1024)S(1)}) custom-call(f32[2048,256]{1,0:T(8,128)} %refs_0_.1, f32[1024,256]{1,0:T(8,128)} %refs_1_.1), custom_call_target="tpu_custom_call" | custom-call | tf_op jit(solution)/shard_map/sinkhorn/pallas_call | solution.py:369
  80.3 0.0 copy-start
  80.3 1.0 copy-done
  81.3 0.0 copy-start.1
  81.3 0.6 copy-done.1
  81.8 33.0 %store.1 = (f32[1024,256]{1,0:T(8,128)}, f32[1024]{0:T(1024)}) custom-call(f32[1024,256]{1,0:T(8,128)} %copy-done, f32[1024]{0:T(1024)} %copy-done.1), custom_call_target="tpu_custom_call" | custom-call | tf_op jit(solution)/shard_map/store/pallas_call | solution.py:404
Async XLA Ops:
  80.3 1.0 copy-start
  81.3 0.6 copy-start.1

commit v7 on v5

--- a/solution.py
+++ b/solution.py
@@ -117,7 +117,6 @@
     def row_wait(n, h, combine):
         rest = z_buf.at[n, h, pl.ds(0, NB - 1)]
         await_bytes(rest, zr.at[2 * n + h])
-        await_bytes(rest, zs.at[2 * n + h])
         return combine([z_buf[n, h, d] for d in range(NB)])
 
     def deep(v, op):
@@ -150,16 +149,14 @@
             lams = []
     row_send(0, 1, jnp.concatenate(lams, axis=0))
 
-    def col_send(n, vec):
-        xy_buf[n, dp] = vec
+    def col_send(n, h, rows):
+        xy_buf[n, h, dp] = jnp.concatenate(rows, axis=0)
         for p in xy_peers:
-            send(xy_buf.at[n, dp], xy_buf.at[n, dp], cs.at[n], cr.at[n], xy_dev(*p))
-
-    def col_wait(n, combine):
-        rest = xy_buf.at[n, pl.ds(0, NDP - 1)]
-        await_bytes(rest, cr.at[n])
-        await_bytes(rest, cs.at[n])
-        return combine([xy_buf[n, d] for d in range(NDP)])
+            send(xy_buf.at[n, h, dp], xy_buf.at[n, h, dp], cs.at[2 * n + h], cr.at[2 * n + h], xy_dev(*p))
+
+    def col_wait(n, h, combine):
+        await_bytes(xy_buf.at[n, h, pl.ds(0, NDP - 1)], cr.at[2 * n + h])
+        return combine([xy_buf[n, h, d] for d in range(NDP)])
 
     def to_row(v, reduce):
         return reduce(v.T, axis=0, keepdims=True)
@@ -180,19 +177,24 @@
         for t in range(8):
             rb_ref[:, HALF * h + 128 * t : HALF * h + 128 * (t + 1)] = vec[t : t + 1, :]
 
-    def row_sums(h, vec=None):
-        acc = [jnp.zeros((8, CH), F32) for _ in groups[h]]
-        for a, r in enumerate(blocks):
-            if vec is not None:
-                wide[r, :] = to_tile(vec[a : a + 1, :])
+    def row_sums(acc, js, h):
+        for r in blocks[4 * h : 4 * h + 4]:
             v = twice(wide[r, :])
-            acc = [t + jnp.sum((mats[j][r, :] * v).reshape(16, 8, CH), axis=0) for t, j in zip(acc, groups[h])]
-        return jnp.concatenate(
-            [jnp.sum(t[:, k : k + 128], axis=0, keepdims=True) for t in acc for k in (0, 128)], axis=0)
-
-    def row_step(n, vec):
-        row_send(n, 0, row_sums(0, vec))
-        row_send(n, 1, row_sums(1))
+            for j in js:
+                acc[j] = acc[j] + jnp.sum((mats[j][r, :] * v).reshape(16, 8, CH), axis=0)
+
+    def row_step(n, column):
+        acc = [jnp.zeros((8, CH), F32) for _ in mats]
+        for h in (0, 1):
+            v = column(h)
+            for a in range(4):
+                wide[blocks[4 * h + a], :] = to_tile(v[a : a + 1, :])
+            if h == 0:
+                row_sums(acc, range(NCH), 0)
+        for h in (0, 1):
+            row_sums(acc, groups[h], 1)
+            row_send(n, h, jnp.concatenate(
+                [jnp.sum(acc[j][:, k : k + 128], axis=0, keepdims=True) for j in groups[h] for k in (0, 128)], axis=0))
 
     def col_terms(r, js):
         return tree([fold(mats[j][r, :] * rb_ref[:, cut(j)], jnp.add) for j in js], jnp.add)
@@ -209,18 +211,19 @@
         row = to_row(jnp.maximum(part[r, :], peak_terms(r, groups[1])), jnp.max)
         rows_of_peaks.append(row)
         peaks[r, :] = to_tile(row)
-    peak = jnp.concatenate(rows_of_peaks, axis=0)
+    peak = [jnp.concatenate(rows_of_peaks[4 * h : 4 * h + 4], axis=0) for h in (0, 1)]
 
     masses = []
-    for r in blocks:
+    for n, r in enumerate(blocks):
         pk = twice(peaks[r, :])
         terms = []
         for j, m in enumerate(mats):
             b = jnp.exp2(m[r, :] - rb_ref[:, cut(j)] - pk)
             m[r, :] = b
             terms.append(fold(b, jnp.add))
-        masses.append(to_row(tree(terms, jnp.add), jnp.sum))
-    col_send(0, peak + jnp.log2(jnp.concatenate(masses, axis=0)))
+        masses.append(rows_of_peaks[n] + jnp.log2(to_row(tree(terms, jnp.add), jnp.sum)))
+        if n % 4 == 3:
+            col_send(0, n // 4, masses[-4:])
 
     def halves(g, carry):
         r = pl.ds(pl.multiple_of(g * 64, 64), 64)
@@ -232,18 +235,26 @@
 
     lax.fori_loop(0, PROT // 64, halves, 0)
 
-    g_log = col_wait(0, log_sum)
-    w = jnp.exp2(peak - g_log)
     ratio = TOTAL_ROWS / TOTAL_PROT
-    row_step(1, w * ratio)
+    g_log, w = [], []
+
+    def first_column(h):
+        g_log.append(col_wait(0, h, log_sum))
+        w.append(jnp.exp2(peak[h] - g_log[h]))
+        return w[h] * ratio
+
+    row_step(1, first_column)
     for a, r in enumerate(blocks):
-        peaks[r, :] = to_tile(w[a : a + 1, :])
+        peaks[r, :] = to_tile(w[a // 4][a % 4 : a % 4 + 1, :])
     spread(0, 1.0 / row_wait(1, 0, total))
     for r in blocks:
         part[r, :] = col_terms(r, groups[0])
     spread(1, 1.0 / row_wait(1, 1, total))
-    col_send(1, w * jnp.concatenate([to_row(part[r, :] + col_terms(r, groups[1]), jnp.sum) for r in blocks], axis=0))
-    row_step(2, w * ratio / col_wait(1, total))
+    for h in (0, 1):
+        rows = [to_row(part[r, :] + col_terms(r, groups[1]), jnp.sum) for r in blocks[4 * h : 4 * h + 4]]
+        col_send(1, h, [w[h][a : a + 1, :] * row for a, row in enumerate(rows)])
+    row_step(2, lambda h: w[h] * ratio / col_wait(1, h, total))
+    w, g_log = jnp.concatenate(w, axis=0), jnp.concatenate(g_log, axis=0)
 
     def scale_rows(h):
         for a in range(8 * h, 8 * h + 8):
@@ -322,23 +333,21 @@
         if p == 1:
             c3x[x] = w * jnp.concatenate([to_row(col_terms(r, range(NCH)), jnp.sum) for r in blocks], axis=0)
             for d in x_peers:
-                send(c3x.at[x], c3x.at[x], cs.at[2], cr.at[2], xy_dev(d, 0))
+                send(c3x.at[x], c3x.at[x], cs.at[4], cr.at[4], xy_dev(d, 0))
 
     scatter_two(1)
-    await_bytes(c3x.at[pl.ds(0, NX - 1)], cr.at[2])
+    await_bytes(c3x.at[pl.ds(0, NX - 1)], cr.at[4])
     c3y[y] = total([c3x[d] for d in range(NX)])
     for d in y_peers:
-        send(c3y.at[y], c3y.at[y], cs.at[3], cr.at[3], xy_dev(0, d))
+        send(c3y.at[y], c3y.at[y], cs.at[5], cr.at[5], xy_dev(0, d))
     scatter_two(2)
     scatter_two(0)
     scatter_two(3)
-    await_bytes(c3y.at[pl.ds(0, NY - 1)], cr.at[3])
+    await_bytes(c3y.at[pl.ds(0, NY - 1)], cr.at[5])
     mass = total([c3y[d] for d in range(NY)])
     pot_ref[...] = ((math.log(TOTAL_ROWS / TOTAL_PROT) - LN2 * g_log) - jnp.log(mass)).reshape(pot_ref.shape)
     for a, r in enumerate(blocks):
         part[r, :] = to_tile(1.0 / mass[a : a + 1, :])
-    await_bytes(c3x.at[pl.ds(0, NX - 1)], cs.at[2])
-    await_bytes(c3y.at[pl.ds(0, NY - 1)], cs.at[3])
     for p in (1, 0, 2, 3):
         gather_one(p)
     for p in (0, 1, 2, 3):
@@ -348,6 +357,13 @@
         await_bytes(out.at[pl.ds(0, size - c1)], fr.at[4 * p + 3])
         for n, sent in enumerate((size - c1, c1 - c2, c1 - c2, size - c1)):
             await_bytes(sums.at[pl.ds(0, sent)], fs.at[4 * p + n])
+
+    for n in range(4):
+        await_bytes(xy_buf.at[n // 2, n % 2, pl.ds(0, NDP - 1)], cs.at[n])
+    for n in range(6):
+        await_bytes(z_buf.at[n // 2, n % 2, pl.ds(0, NB - 1)], zs.at[n])
+    await_bytes(c3x.at[pl.ds(0, NX - 1)], cs.at[4])
+    await_bytes(c3y.at[pl.ds(0, NY - 1)], cs.at[5])
 
 
 def body(embeddings, prototypes):
@@ -377,13 +393,13 @@
             vm((ROWS, DW), BF16),
             vm((1, ROWS), F32),
             vm((3, 2, NB, 8, 128), F32),
-            vm((2, NDP, 8, 128), F32),
+            vm((2, 2, NDP, 4, 128), F32),
             vm((NX, 8, 128), F32),
             vm((NY, 8, 128), F32),
             vm((PROT, DW), F32),
             dma((NCH + PROT // CH,)),
             dma((6,)), dma((6,)),
-            dma((4,)), dma((4,)),
+            dma((6,)), dma((6,)),
             dma((4 * len(PARTS),)), dma((4 * len(PARTS),)), dma((NY * len(PARTS),)),
         ],
         compiler_params=pltpu.CompilerParams(

time: 82 us -> 81.6 us (level)
  no operation moved by 1% of the time
where the time goes in v7:
time: 81.6 us; the launch traced here: 81.4 us
  Pallas kernels  79.2 us (97%)
  local copies, waits for them, and re-layouts  1.57 us (2%)
    pallas_call x1, Pallas kernels, body(): pl.pallas_call(kernel, out_shape=(pltpu.VMEM((PROT, DW), F32), pltpu.VMEM...  79.2 us

profile of v7, /device:TPU:1, one launch (start us, length us, event | category | flops | bytes accessed | tf_op | source)
XLA Modules:
  0.0 81.4 jit_solution(11242981269916223971)
XLA Ops:
  0.6 79.2 %sinkhorn.1 = (f32[1024,256]{1,0:T(8,128)S(1)}, f32[1024]{0:T(1024)S(1)}) custom-call(f32[2048,256]{1,0:T(8,128)} %refs_0_.1, f32[1024,256]{1,0:T(8,128)} %refs_1_.1), custom_call_target="tpu_custom_call" | custom-call | tf_op jit(solution)/shard_map/sinkhorn/pallas_call | solution.py:374
  79.9 1.0 %copy.6 = f32[1024,256]{1,0:T(8,128)} copy(f32[1024,256]{1,0:T(8,128)S(1)} %get-tuple-element.2) | data formatting | bytes 2097152
  80.9 0.6 copy.7

commit v8 on v7

--- a/solution.py
+++ b/solution.py
@@ -65,7 +65,7 @@
 
 
 def kernel(*refs):
-    (e_hbm, p_hbm, out, pot_ref, e_ref, p_ref, p3_ref), refs = refs[:7], refs[7:]
+    (e_hbm, p_hbm, out, peak_ref, mass_ref, e_ref, p_ref, p3_ref), refs = refs[:8], refs[8:]
     mats, refs = refs[:NCH], refs[NCH:]
     b1s, refs = refs[: len(PARTS)], refs[len(PARTS) :]
     mids, refs = refs[: len(PARTS)], refs[len(PARTS) :]
@@ -330,7 +330,7 @@
         acc = sums[rows, :] + product(rows, half(1)) if p == 0 else product(rows, slice(0, ROWS))
         sums[rows, :] = acc * twice(peaks[rows, :])
         scatter_one(p)
-        if p == 1:
+        if p == 2:
             c3x[x] = w * jnp.concatenate([to_row(col_terms(r, range(NCH)), jnp.sum) for r in blocks], axis=0)
             for d in x_peers:
                 send(c3x.at[x], c3x.at[x], cs.at[4], cr.at[4], xy_dev(d, 0))
@@ -345,7 +345,8 @@
     scatter_two(3)
     await_bytes(c3y.at[pl.ds(0, NY - 1)], cr.at[5])
     mass = total([c3y[d] for d in range(NY)])
-    pot_ref[...] = ((math.log(TOTAL_ROWS / TOTAL_PROT) - LN2 * g_log) - jnp.log(mass)).reshape(pot_ref.shape)
+    peak_ref[...] = (LN2 * g_log).reshape(peak_ref.shape)
+    mass_ref[...] = jnp.log(mass).reshape(mass_ref.shape)
     for a, r in enumerate(blocks):
         part[r, :] = to_tile(1.0 / mass[a : a + 1, :])
     for p in (1, 0, 2, 3):
@@ -371,11 +372,11 @@
     dma = pltpu.SemaphoreType.DMA
     counts = [(NX, NY) if first == "x" else (NY, NX) for _, _, first in PARTS]
     sizes = [size for _, size, _ in PARTS]
-    new_protos, pot = pl.pallas_call(
+    new_protos, peak, mass = pl.pallas_call(
         kernel,
-        out_shape=(pltpu.VMEM((PROT, DW), F32), pltpu.VMEM((PROT,), F32)),
+        out_shape=(pltpu.VMEM((PROT, DW), F32), pltpu.VMEM((PROT,), F32), pltpu.VMEM((PROT,), F32)),
         in_specs=[pl.BlockSpec(memory_space=pl.ANY)] * 2,
-        out_specs=(pl.BlockSpec(memory_space=vm), pl.BlockSpec(memory_space=vm)),
+        out_specs=(pl.BlockSpec(memory_space=vm),) * 3,
         scratch_shapes=[
             vm((ROWS, DW), F32),
             vm((PROT, DW), F32),
@@ -406,7 +407,7 @@
             collective_id=0, has_side_effects=True, vmem_limit_bytes=56 * 1024 * 1024),
         name="sinkhorn",
     )(embeddings, prototypes)
-    return new_protos, pot
+    return new_protos, (math.log(TOTAL_ROWS / TOTAL_PROT) - peak) - mass
 
 
 def solution(mesh):

time: 81.6 us -> 81.9 us (level)
  no operation moved by 1% of the time
where the time goes in v8:
time: 81.9 us; the launch traced here: 81.8 us
  Pallas kernels  79.6 us (97%)
  local copies, waits for them, and re-layouts  0.97 us (1%)
    pallas_call x1, Pallas kernels, body(): pl.pallas_call(kernel, out_shape=(pltpu.VMEM((PROT, DW), F32), pltpu.VMEM...  79.6 us

profile of v8, /device:TPU:1, one launch (start us, length us, event | category | flops | bytes accessed | tf_op | source)
XLA Modules:
  0.0 81.8 jit_solution(10911846252378198938)
XLA Ops:
  0.6 79.6 %sinkhorn.1 = (f32[1024,256]{1,0:T(8,128)S(1)}, f32[1024]{0:T(1024)S(1)}, f32[1024]{0:T(1024)S(1)}) custom-call(f32[2048,256]{1,0:T(8,128)} %refs_0_.1, f32[1024,256]{1,0:T(8,128)} %refs_1_.1), custom_call_target="tpu_custom_call" | custom-call | tf_op jit(solution)/shard_map/sinkhorn/pallas_call | solution.py:375
  80.2 0.6 subtract_subtract_fusion
  80.8 1.0 %copy.5 = f32[1024,256]{1,0:T(8,128)} copy(f32[1024,256]{1,0:T(8,128)S(1)} %get-tuple-element.8) | data formatting | bytes 2097152

commit v9 on v7

--- a/solution.py
+++ b/solution.py
@@ -330,7 +330,7 @@
         acc = sums[rows, :] + product(rows, half(1)) if p == 0 else product(rows, slice(0, ROWS))
         sums[rows, :] = acc * twice(peaks[rows, :])
         scatter_one(p)
-        if p == 1:
+        if p == 2:
             c3x[x] = w * jnp.concatenate([to_row(col_terms(r, range(NCH)), jnp.sum) for r in blocks], axis=0)
             for d in x_peers:
                 send(c3x.at[x], c3x.at[x], cs.at[4], cr.at[4], xy_dev(d, 0))
@@ -340,8 +340,8 @@
     c3y[y] = total([c3x[d] for d in range(NX)])
     for d in y_peers:
         send(c3y.at[y], c3y.at[y], cs.at[5], cr.at[5], xy_dev(0, d))
+    scatter_two(0)
     scatter_two(2)
-    scatter_two(0)
     scatter_two(3)
     await_bytes(c3y.at[pl.ds(0, NY - 1)], cr.at[5])
     mass = total([c3y[d] for d in range(NY)])
@@ -350,7 +350,7 @@
         part[r, :] = to_tile(1.0 / mass[a : a + 1, :])
     for p in (1, 0, 2, 3):
         gather_one(p)
-    for p in (0, 1, 2, 3):
+    for p in (1, 2, 3, 0):
         gather_two(p)
     for p in (0, 1, 2, 3):
         _, size, _, _, c1, c2 = plan(p)

time: 81.6 us -> 83.1 us (1.018)
  Pallas kernels: 79.2 us -> 80.5 us
    pallas_call x1, Pallas kernels: 79.2 us -> 80.5 us  [body(): pl.pallas_call(kernel, out_shape=(pltpu.VMEM((PROT, DW), F32), pltpu.VMEM...]
where the time goes in v9:
time: 83.1 us; the launch traced here: 82.7 us
  Pallas kernels  80.5 us (97%)
  local copies, waits for them, and re-layouts  1.57 us (2%)
    pallas_call x1, Pallas kernels, body(): pl.pallas_call(kernel, out_shape=(pltpu.VMEM((PROT, DW), F32), pltpu.VMEM...  80.5 us

profile of v9, /device:TPU:1, one launch (start us, length us, event | category | flops | bytes accessed | tf_op | source)
XLA Modules:
  0.0 82.7 jit_solution(7633217076436228168)
XLA Ops:
  0.6 80.5 %sinkhorn.1 = (f32[1024,256]{1,0:T(8,128)S(1)}, f32[1024]{0:T(1024)S(1)}) custom-call(f32[2048,256]{1,0:T(8,128)} %refs_0_.1, f32[1024,256]{1,0:T(8,128)} %refs_1_.1), custom_call_target="tpu_custom_call" | custom-call | tf_op jit(solution)/shard_map/sinkhorn/pallas_call | solution.py:374
  81.2 1.0 %copy.6 = f32[1024,256]{1,0:T(8,128)} copy(f32[1024,256]{1,0:T(8,128)S(1)} %get-tuple-element.2) | data formatting | bytes 2097152
  82.1 0.6 copy.7

commit v10 on v7

--- a/solution.py
+++ b/solution.py
@@ -350,7 +350,7 @@
         part[r, :] = to_tile(1.0 / mass[a : a + 1, :])
     for p in (1, 0, 2, 3):
         gather_one(p)
-    for p in (0, 1, 2, 3):
+    for p in (1, 0, 2, 3):
         gather_two(p)
     for p in (0, 1, 2, 3):
         _, size, _, _, c1, c2 = plan(p)

time: 81.6 us -> 81.6 us (level)
  no operation moved by 1% of the time
where the time goes in v10:
time: 81.6 us; the launch traced here: 81.5 us
  Pallas kernels  79.3 us (97%)
  local copies, waits for them, and re-layouts  1.57 us (2%)
    pallas_call x1, Pallas kernels, body(): pl.pallas_call(kernel, out_shape=(pltpu.VMEM((PROT, DW), F32), pltpu.VMEM...  79.3 us

profile of v10, /device:TPU:1, one launch (start us, length us, event | category | flops | bytes accessed | tf_op | source)
XLA Modules:
  0.0 81.5 jit_solution(16750859383422646340)
XLA Ops:
  0.6 79.3 %sinkhorn.1 = (f32[1024,256]{1,0:T(8,128)S(1)}, f32[1024]{0:T(1024)S(1)}) custom-call(f32[2048,256]{1,0:T(8,128)} %refs_0_.1, f32[1024,256]{1,0:T(8,128)} %refs_1_.1), custom_call_target="tpu_custom_call" | custom-call | tf_op jit(solution)/shard_map/sinkhorn/pallas_call | solution.py:374
  79.9 1.0 %copy.6 = f32[1024,256]{1,0:T(8,128)} copy(f32[1024,256]{1,0:T(8,128)S(1)} %get-tuple-element.2) | data formatting | bytes 2097152
  80.9 0.6 copy.7
